TPU v7x, 256 devices: a whole 4x4x8 slice. The times are simulated.
256 devices in a mesh: pipe: 8 (over y, x_lo), expert: 32 (over z, x_hi, core).
Axes of the slice: x: 4 (x_hi: 2, x_lo: 2; x = x_hi * 2 + x_lo), y: 4, z: 8, core: 2. Of those that a mesh axis runs over, the one named last changes fastest.
Arguments:
- forward_input: bfloat16 [8, 4096, 3584], P('pipe', 'expert'), may hold values from -6 to 6
- forward_route: int32 [8, 4096, 1], P('pipe', 'expert'), may hold values from 0 to 7; in each aligned block of 128 rows (0 to 127, 128 to 255, ..., all dimensions but the last counted through in order) at most 32 rows name the same one
- forward_weight: float32 [8, 4096], P('pipe', 'expert'), may hold values from 0.2 to 1
- section_gradient: bfloat16 [8, 4096, 3584], P('pipe', 'expert'), may hold values from -6 to 6
- backward_route: int32 [8, 4096, 1], P('pipe', 'expert'), may hold values from 0 to 7; in each aligned block of 128 rows (0 to 127, 128 to 255, ..., all dimensions but the last counted through in order) at most 32 rows name the same one
- backward_weight: float32 [8, 4096], P('pipe', 'expert'), may hold values from 0.2 to 1
- saved_gate: bfloat16 [8, 32, 32, 32, 256], P('pipe', 'expert'), may hold values from -6 to 6
- saved_up: bfloat16 [8, 32, 32, 32, 256], P('pipe', 'expert'), may hold values from -6 to 6
- gate_weight: bfloat16 [8, 32, 3584, 256], P('pipe', 'expert'), may hold values from -0.09375 to 0.09375
- up_weight: bfloat16 [8, 32, 3584, 256], P('pipe', 'expert'), may hold values from -0.09375 to 0.09375
- down_weight: bfloat16 [8, 32, 256, 3584], P('pipe', 'expert'), may hold values from -0.1875 to 0.1875
Outputs:
- forward_output: bfloat16 [8, 4096, 3584], P('pipe', 'expert')
- input_gradient: bfloat16 [8, 4096, 3584], P('pipe', 'expert')
- weight_gradient: float32 [8, 4096], P('pipe', 'expert')
Inputs may be any that keep to these rules, and one draw needn't show every extreme that they name: `forward_route`: in each device's block of 128 tokens no expert is named by more than 32 tokens, a bound that some block reaches. `backward_route`: in each device's block of 128 tokens no expert is named by more than 32 tokens, a bound that some block reaches.
All inputs are finite; a program needn't handle non-finite values.
Results may differ from a plain program's by a relative error of at most 0.012.
Values may be sent and summed in bfloat16 or wider, within the bound.
No kernel may reach another device: no remote copies, remote signals or barrier semaphores. Data moves between devices by JAX's collectives and lax.ppermute only.
A program may use at most 128 MiB of HBM per device.

v0:
```python
import jax
import jax.numpy as jnp
from jax import lax
from jax.sharding import PartitionSpec as P

WS = 4
AXES = ("pipe", "expert")


def places(index, slices):
    section, place = divmod(index, slices)
    return section, place // WS, place // 2 % 2, place % 2


def send(value, to):
    sections, slices = lax.axis_size("pipe"), lax.axis_size("expert")
    planes = slices // WS
    pairs = []
    for index in range(sections * slices):
        section, plane, half, core = to(*places(index, slices))
        target = (section % sections) * slices + (plane % planes) * WS + half * 2 + core
        pairs.append((index, target))
    return lax.ppermute(value, AXES, pairs)


def shift(value, by):
    return send(value, lambda s, z, h, c: (s + by, z, h, c))


def onward(value, by):
    return send(value, lambda s, z, h, c: (s + s % 2 * 2, z + by, h, c))


def across(value, far):
    return send(value, lambda s, z, h, c: (s + 1 - s % 2 * 2, z, h ^ far, c))


def swap_half(value):
    return send(value, lambda s, z, h, c: (s, z, 1 - h, c))


def swap_core(value):
    return send(value, lambda s, z, h, c: (s, z, h, 1 - c))


def dot(a, b):
    return jnp.dot(a, b, preferred_element_type=jnp.float32)


def dot_last(a, b):
    return lax.dot_general(a, b, (((1,), (1,)), ((), ())), preferred_element_type=jnp.float32)


def keys_of(routes, planes, capacity):
    labels = jnp.arange(planes, dtype=jnp.int32)
    onehot = (routes[:, None] == labels[None, :]).astype(jnp.int32)
    before = jnp.cumsum(onehot, axis=0) - onehot
    within = jnp.sum(before * onehot, axis=1)
    return routes * capacity + within


def pack(values, keys, slots):
    onehot = (jnp.arange(slots, dtype=jnp.int32)[:, None] == keys[None, :]).astype(jnp.bfloat16)
    return dot(onehot, values).astype(jnp.bfloat16)


def unpack(rows, keys):
    onehot = (keys[:, None] == jnp.arange(rows.shape[0], dtype=jnp.int32)[None, :]).astype(jnp.bfloat16)
    return dot(onehot, rows)


def exchange(rows, planes):
    groups = [[plane * WS + place for plane in range(planes)] for place in range(WS)]
    return lax.all_to_all(rows, "expert", 0, 0, axis_index_groups=groups, tiled=True)


def per_device(
    forward_input,
    forward_route,
    forward_weight,
    section_gradient,
    backward_route,
    backward_weight,
    saved_gate,
    saved_up,
    gate_weight,
    up_weight,
    down_weight,
):
    slices = lax.axis_size("expert")
    planes = slices // WS
    capacity = saved_gate.shape[3]
    slots = planes * capacity
    place = lax.axis_index("expert")
    half, core = place // 2 % 2, place % 2

    gate_own, up_own, down_own = gate_weight[0, 0], up_weight[0, 0], down_weight[0, 0]
    onward_route = shift(forward_route[0, :, 0], -1)
    upstream = shift(section_gradient[0], -1)

    forward_keys = keys_of(forward_route[0, :, 0], planes, capacity)
    backward_keys = keys_of(backward_route[0, :, 0], planes, capacity)
    plane = place // WS
    onward_keys = keys_of((onward_route - plane + planes) % planes, planes, capacity)
    packed = pack(forward_input[0], onward_keys, slots)
    order = [distance for pair in zip(range(planes // 2, planes), range(planes // 2 - 1, -1, -1)) for distance in pair]
    arrived = {d: onward(packed[d * capacity:(d + 1) * capacity], d) for d in order}
    forward_rows = jnp.concatenate([arrived[d] for d in range(planes)], axis=0)

    turns = jnp.arange(planes, dtype=jnp.int32) * WS
    mine = jnp.concatenate([turns + half * 2 + core, turns + (1 - half) * 2 + core])
    other = jnp.concatenate([turns + half * 2 + 1 - core, turns + (1 - half) * 2 + 1 - core])
    saved = jnp.concatenate([saved_gate[0, 0], saved_up[0, 0]], axis=2)
    saved_own, saved_next = saved[mine].reshape(2 * slots, -1), saved[other].reshape(2 * slots, -1)

    down_far = swap_half(down_own)
    backward_packed = pack(upstream, backward_keys, slots)
    forward_rows, backward_packed, down_far, gate_own, up_own, saved_next, saved_own, forward_first = lax.optimization_barrier(
        (forward_rows, backward_packed, down_far, gate_own, up_own, saved_next, saved_own, forward_input[0])
    )

    far_rows, near_rows = across(forward_rows, 1), across(forward_rows, 0)
    saved_next = swap_core(saved_next)
    saved_next, backward_packed, gate_own, up_own, down_own, down_far = lax.optimization_barrier(
        (saved_next, backward_packed, gate_own, up_own, down_own, down_far)
    )
    backward_rows = exchange(backward_packed, planes)
    gates = jnp.concatenate([gate_own, swap_core(gate_own), up_own, swap_core(up_own)], axis=1)
    down = jnp.concatenate([down_own, swap_core(down_own), down_far, swap_core(down_far)], axis=0)
    near = down.shape[0] // 2
    units = near // 2
    g = jnp.concatenate([saved_own[:, :units], saved_next[:, :units]], axis=1)
    u = jnp.concatenate([saved_own[:, units:], saved_next[:, units:]], axis=1)

    def hidden_of(rows):
        both = dot(rows, gates)
        gate, upper = both[:, :near], both[:, near:]
        return (gate * jax.nn.sigmoid(gate) * upper).astype(jnp.bfloat16)

    far_hidden = hidden_of(far_rows)
    far_hidden, forward_first = lax.optimization_barrier((far_hidden, forward_first))
    far_hidden = swap_half(far_hidden)
    inputs = shift(forward_first, 1)
    hidden = jnp.concatenate([hidden_of(near_rows), far_hidden], axis=1)
    turned = (plane - jnp.arange(planes, dtype=jnp.int32) + planes) % planes
    hidden = jnp.take(hidden.reshape(planes, capacity, -1), turned, axis=0).reshape(slots, -1)
    returned = exchange(dot(hidden, down).astype(jnp.bfloat16), planes)
    mixed = unpack(returned, forward_keys)
    forward_output = (inputs.astype(jnp.float32) + forward_weight[0][:, None] * mixed).astype(jnp.bfloat16)

    back_far = swap_half(dot_last(backward_rows, down[near:]).astype(jnp.bfloat16))
    back_near = dot_last(backward_rows, down[:near])

    def back_of(back_r, gate, upper):
        gate, upper = gate.astype(jnp.float32), upper.astype(jnp.float32)
        sigma = jax.nn.sigmoid(gate)
        active = gate * sigma
        saved_hidden = (active * upper).astype(jnp.bfloat16).astype(jnp.float32)
        share = jnp.sum(back_r * saved_hidden, axis=1)
        d_gate = (back_r * upper * sigma * (1.0 + gate * (1.0 - sigma))).astype(jnp.bfloat16)
        d_up = (back_r * active).astype(jnp.bfloat16)
        return dot_last(jnp.concatenate([d_gate, d_up], axis=1), gates), share

    far_part, far_share = back_of(back_far.astype(jnp.float32), g[slots:], u[slots:])
    far_part = swap_half(far_part.astype(jnp.bfloat16))
    far_share = swap_half(far_share)
    near_part, near_share = back_of(back_near, g[:slots], u[:slots])
    part = (near_part + far_part.astype(jnp.float32)).astype(jnp.bfloat16)
    rest, terms = near_share + far_share, []
    for _ in range(3):
        terms.append(rest.astype(jnp.bfloat16))
        rest = rest - terms[-1].astype(jnp.float32)
    width = part.shape[1]
    column = jnp.arange(128, dtype=jnp.int32)[None, :]
    tail = sum(jnp.where(column == n, term[:, None], jnp.bfloat16(0)) for n, term in enumerate(terms))
    returned = exchange(jnp.concatenate([part, tail], axis=1), planes)
    mixed = unpack(returned, backward_keys)
    weight_gradient = jnp.sum(mixed[:, width:], axis=1)
    mixed = mixed[:, :width]
    input_gradient = (upstream.astype(jnp.float32) + backward_weight[0][:, None] * mixed).astype(jnp.bfloat16)
    return (forward_output[None], input_gradient[None], weight_gradient[None])


def solution(mesh):
    placed = (
        P("pipe", "expert", None),
        P("pipe", "expert", None),
        P("pipe", "expert"),
        P("pipe", "expert", None),
        P("pipe", "expert", None),
        P("pipe", "expert"),
        P("pipe", "expert", None, None, None),
        P("pipe", "expert", None, None, None),
        P("pipe", "expert", None, None),
        P("pipe", "expert", None, None),
        P("pipe", "expert", None, None),
    )
    return jax.shard_map(
        per_device,
        mesh=mesh,
        in_specs=placed,
        out_specs=(P("pipe", "expert", None), P("pipe", "expert", None), P("pipe", "expert")),
        check_vma=False,
    )
```

profile of v0, /device:TPU:2, one launch (start us, length us, event | category | flops | bytes accessed | tf_op | source)
XLA Modules:
  0.0 273.0 jit_solution(4196038016511876436)
XLA Ops:
  0.6 2.3 collective-permute-start
  3.0 2.2 collective-permute-start.9
  5.2 2.1 collective-permute-start.10
  18.7 4.3 %collective-permute-start.3 = (bf16[32,3584]{1,0:T(8,128)(2,1)S(1)}, bf16[32,3584]{1,0:T(8,128)(2,1)S(1)}, u32[]{:S(2)}, u32[]{:S(2)}) collective-permute-start(bf16[32,3584]{1,0:T(8,128)(2,1)S(1)} %get-tuple-element.42), channel_id=1, source_target_pairs={{0,8},{1,9},{2,10},{3,11},{4,12},{5,13},{6,14},{7,15},{8,16},{9,17... | collective-permute-start | bytes 688136 | tf_op jit(solution)/shard_map/ppermute | solution.py:23
  23.0 8.1 %collective-permute-start.4 = (bf16[32,3584]{1,0:T(8,128)(2,1)S(1)}, bf16[32,3584]{1,0:T(8,128)(2,1)S(1)}, u32[]{:S(2)}, u32[]{:S(2)}) collective-permute-start(bf16[32,3584]{1,0:T(8,128)(2,1)S(1)} %get-tuple-element.41), channel_id=1, source_target_pairs={{0,12},{1,13},{2,14},{3,15},{4,16},{5,17},{6,18},{7,19},{8,20},{9,... | collective-permute-start | bytes 688136 | tf_op jit(solution)/shard_map/ppermute | solution.py:23
  33.9 5.5 %collective-permute-start.5 = (bf16[32,3584]{1,0:T(8,128)(2,1)S(1)}, bf16[32,3584]{1,0:T(8,128)(2,1)S(1)}, u32[]{:S(2)}, u32[]{:S(2)}) collective-permute-start(bf16[32,3584]{1,0:T(8,128)(2,1)S(1)} %get-tuple-element.40), channel_id=1, source_target_pairs={{0,16},{1,17},{2,18},{3,19},{4,20},{5,21},{6,22},{7,23},{8,24},{9,... | collective-permute-start | bytes 688136 | tf_op jit(solution)/shard_map/ppermute | solution.py:23
  39.3 9.2 %collective-permute-done.3 = bf16[32,3584]{1,0:T(8,128)(2,1)S(1)} collective-permute-done((bf16[32,3584]{1,0:T(8,128)(2,1)S(1)}, bf16[32,3584]{1,0:T(8,128)(2,1)S(1)}, u32[]{:S(2)}, u32[]{:S(2)}) %collective-permute-start.3) | collective-permute-done | bytes 229408 | tf_op jit(solution)/shard_map/ppermute | solution.py:23
  48.5 13.2 %collective-permute-done.4 = bf16[32,3584]{1,0:T(8,128)(2,1)S(1)} collective-permute-done((bf16[32,3584]{1,0:T(8,128)(2,1)S(1)}, bf16[32,3584]{1,0:T(8,128)(2,1)S(1)}, u32[]{:S(2)}, u32[]{:S(2)}) %collective-permute-start.4) | collective-permute-done | bytes 229408 | tf_op jit(solution)/shard_map/ppermute | solution.py:23
  61.8 6.9 %collective-permute-start.7 = (bf16[32,3584]{1,0:T(8,128)(2,1)}, bf16[32,3584]{1,0:T(8,128)(2,1)S(1)}, u32[]{:S(2)}, u32[]{:S(2)}) collective-permute-start(bf16[32,3584]{1,0:T(8,128)(2,1)} %get-tuple-element.38), channel_id=1, source_target_pairs={{0,24},{1,25},{2,26},{3,27},{4,28},{5,29},{6,30},{7,31},{8,0},{9,1... | collective-permute-start | bytes 688136 | tf_op jit(solution)/shard_map/ppermute | solution.py:23
  68.8 7.0 %collective-permute-done.7 = bf16[32,3584]{1,0:T(8,128)(2,1)S(1)} collective-permute-done((bf16[32,3584]{1,0:T(8,128)(2,1)}, bf16[32,3584]{1,0:T(8,128)(2,1)S(1)}, u32[]{:S(2)}, u32[]{:S(2)}) %collective-permute-start.7) | collective-permute-done | bytes 229408 | tf_op jit(solution)/shard_map/ppermute | solution.py:23
  83.2 2.5 collective-permute-start.16
  86.5 2.9 %constant_dynamic-update-slice_fusion.11 = bf16[3584,1024]{1,0:T(8,128)(2,1)} fusion(bf16[3584,256]{1,0:T(8,128)(2,1)} %bitcast.5), kind=kLoop, calls=%fused_computation.118 | loop fusion | bytes 3670016
  89.9 7.6 %all-to-all-start.1 = ((bf16[8,32,3584]{2,1,0:T(8,128)(2,1)}), bf16[8,32,3584]{2,1,0:T(8,128)(2,1)}, u32[]{:S(2)}, u32[]{:S(2)}) async-start(bf16[8,32,3584]{2,1,0:T(8,128)(2,1)} %bitcast.25), calls=%async_computation.1 | async-start | bytes 3670016 | tf_op jit(solution)/shard_map/all_to_all | solution.py:74
  99.4 3.0 %constant_dynamic-update-slice_fusion.10 = bf16[3584,1024]{1,0:T(8,128)(2,1)} fusion(bf16[3584,1024]{1,0:T(8,128)(2,1)} %constant_dynamic-update-slice_fusion.11, bf16[3584,256]{1,0:T(8,128)(2,1)} %collective-permute-done.13), kind=kLoop, calls=%fused_computation.117 | loop fusion | bytes 3670016
  103.8 2.9 %constant_dynamic-update-slice_fusion.8 = bf16[3584,1024]{1,0:T(8,128)(2,1)} fusion(bf16[3584,1024]{1,0:T(8,128)(2,1)} %constant_dynamic-update-slice_fusion.9, bf16[3584,256]{1,0:T(8,128)(2,1)} %collective-permute-done.14), kind=kLoop, calls=%fused_computation.115 | loop fusion | bytes 3670016 | tf_op jit(solution)/shard_map/concatenate | solution.py:128
  106.7 19.1 %collective-permute-done.11 = bf16[256,3584]{1,0:T(8,128)(2,1)} collective-permute-done((bf16[256,3584]{1,0:T(8,128)(2,1)}, bf16[256,3584]{1,0:T(8,128)(2,1)}, u32[]{:S(2)}, u32[]{:S(2)}) %collective-permute-start.11) | collective-permute-done | bytes 1835040 | tf_op jit(solution)/shard_map/ppermute | solution.py:23
  125.8 5.7 %fusion.81 = f32[256,1024]{1,0:T(8,128)S(1)} fusion(bf16[256,3584]{1,0:T(8,128)(2,1)} %collective-permute-done.11, bf16[3584,1024]{1,0:T(8,128)(2,1)} %constant_dynamic-update-slice_fusion.8), kind=kOutput, calls=%fused_computation.168 | convolution fusion | flops 1879048192 | bytes 10223616 | tf_op jit(solution)/shard_map/dot_general | solution.py:47
  131.7 2.7 collective-permute-start.17
  134.3 3.6 %fusion.82 = f32[256,1024]{1,0:T(8,128)S(1)} fusion(bf16[256,3584]{1,0:T(8,128)(2,1)} %collective-permute-done.16, bf16[3584,1024]{1,0:T(8,128)(2,1)S(1)} %copy-done.5), kind=kOutput, calls=%fused_computation.169 | convolution fusion | flops 1879048192 | bytes 10223616 | tf_op jit(solution)/shard_map/dot_general | solution.py:47
  138.1 3.0 %collective-permute-done.17 = bf16[256,512]{1,0:T(8,128)(2,1)S(1)} collective-permute-done((bf16[256,512]{1,0:T(8,128)(2,1)S(1)}, bf16[256,512]{1,0:T(8,128)(2,1)S(1)}, u32[]{:S(2)}, u32[]{:S(2)}) %collective-permute-start.17) | collective-permute-done | bytes 262176 | tf_op jit(solution)/shard_map/ppermute | solution.py:23
  143.4 4.6 %fusion.22 = bf16[256,512]{1,0:T(8,128)(2,1)} fusion(bf16[256,3584]{1,0:T(8,128)(2,1)} %bitcast.26, bf16[256,3584]{1,0:T(8,128)(2,1)} %collective-permute-done.19, bf16[256,3584]{1,0:T(8,128)(2,1)} %collective-permute-done.10), kind=kOutput, calls=%fused_computation.31 | convolution fusion | flops 946995200 | bytes 5767168 | tf_op jit(solution)/shard_map/dot_general | solution.py:51
  149.0 5.0 %fusion.8 = bf16[256,3584]{1,0:T(8,128)(2,1)} fusion(bf16[256,1024]{1,0:T(8,128)(2,1)S(1)} %bitcast_select_fusion, bf16[256,3584]{1,0:T(8,128)(2,1)} %collective-permute-done.19, bf16[256,3584]{1,0:T(8,128)(2,1)} %collective-permute-done.10, bf16[256,3584]{1,0:T(8,128)(2,1)} %collective-permute-done.18, bf16[256,3584]{1,0:T(8,128)(2,1)S(1)} %bitcast.81), kind=kOutput, calls=%fused_computation.12 | convolution fusion | flops 1909325824 | bytes 9699328 | tf_op jit(solution)/shard_map/dot_general | solution.py:47
  154.0 7.7 %all-to-all-start = ((bf16[8,32,3584]{2,1,0:T(8,128)(2,1)}), bf16[8,32,3584]{2,1,0:T(8,128)(2,1)S(1)}, u32[]{:S(2)}, u32[]{:S(2)}) async-start(bf16[8,32,3584]{2,1,0:T(8,128)(2,1)} %bitcast.63), calls=%async_computation | async-start | bytes 3670016 | tf_op jit(solution)/shard_map/all_to_all | solution.py:74
  161.7 4.3 %fusion.40 = (f32[256]{0:T(256)S(1)}, f32[256]{0:T(256)S(1)}, bf16[256,512]{1,0:T(8,128)(2,1)S(1)}, bf16[256,512]{1,0:T(8,128)(2,1)S(1)}, f32[256,512]{1,0:T(8,128)S(1)}) fusion(bf16[256,512]{1,0:T(8,128)(2,1)} %collective-permute-done.20, bf16[512,256]{1,0:T(8,128)(2,1)} %get-tuple-element.52, bf16[512,256]{1,0:T(8,128)(2,1)S(1)} %copy-done.6, ...), kind=kOutput, calls=%fused_computation.60 | convolution fusion | flops 954727936 | bytes 7866368 | tf_op jit(solution)/shard_map/dot_general | solution.py:51
  167.5 5.4 %convolution_convert_fusion = bf16[256,3584]{1,0:T(8,128)(2,1)S(1)} fusion(bf16[3584,1024]{1,0:T(8,128)(2,1)} %constant_dynamic-update-slice_fusion.8, bf16[256,512]{1,0:T(8,128)(2,1)S(1)} %get-tuple-element.48, bf16[256,512]{1,0:T(8,128)(2,1)S(1)} %get-tuple-element.46), kind=kOutput, calls=%fused_computation.13 | convolution fusion | flops 1881014272 | bytes 9699328 | tf_op jit(solution)/shard_map/dot_general | solution.py:51
  174.1 2.6 collective-permute-start.22
  176.8 38.0 %collective-permute-done.22 = f32[256]{0:T(256)S(1)} collective-permute-done((f32[256]{0:T(256)S(1)}, f32[256]{0:T(256)S(1)}, u32[]{:S(2)}, u32[]{:S(2)}) %collective-permute-start.22) | collective-permute-done | bytes 1056 | tf_op jit(solution)/shard_map/ppermute | solution.py:23
  215.0 2.1 fusion.11
  219.7 6.9 %all-to-all-start.2 = ((bf16[8,32,3712]{2,1,0:T(8,128)(2,1)}), bf16[8,32,3712]{2,1,0:T(8,128)(2,1)S(1)}, u32[]{:S(2)}, u32[]{:S(2)}) async-start(bf16[8,32,3712]{2,1,0:T(8,128)(2,1)} %bitcast.27), calls=%async_computation.2 | async-start | bytes 3801088 | tf_op jit(solution)/shard_map/all_to_all | solution.py:74
  227.1 18.7 %collective-permute-done.15 = bf16[128,3584]{1,0:T(8,128)(2,1)} collective-permute-done((bf16[128,3584]{1,0:T(8,128)(2,1)}, bf16[128,3584]{1,0:T(8,128)(2,1)}, u32[]{:S(2)}, u32[]{:S(2)}) %collective-permute-start.15) | collective-permute-done | bytes 917536 | tf_op jit(solution)/shard_map/ppermute | solution.py:23
  245.8 3.1 %fusion.25 = bf16[1,128,3584]{2,1,0:T(8,128)(2,1)} fusion(bf16[128,3584]{1,0:T(8,128)(2,1)} %collective-permute-done.15, bf16[256,3584]{1,0:T(8,128)(2,1)} %bitcast.58, f32[128]{0:T(128)S(1)} %bitcast.75, s32[128]{0:T(128)S(1)} %multiply_add_fusion), kind=kOutput, calls=%fused_computation.33 | convolution fusion | flops 236748800 | bytes 3671040 | tf_op jit(solution)/shard_map/dot_general | solution.py:47
  248.9 21.8 %all-to-all-done.2 = bf16[8,32,3712]{2,1,0:T(8,128)(2,1)S(1)} async-done(((bf16[8,32,3712]{2,1,0:T(8,128)(2,1)}), bf16[8,32,3712]{2,1,0:T(8,128)(2,1)S(1)}, u32[]{:S(2)}, u32[]{:S(2)}) %all-to-all-start.2) | async-done | bytes 1900576 | tf_op jit(solution)/shard_map/all_to_all | solution.py:74
  (117 shorter events, 38.1 us)
Async XLA Ops:
  0.6 9.9 %collective-permute-start = (s32[128]{0:T(128)}, s32[128]{0:T(128)S(1)}, u32[]{:S(2)}, u32[]{:S(2)}) collective-permute-start(s32[128]{0:T(128)} %bitcast.72), channel_id=1, source_target_pairs={{0,224},{1,225},{2,226},{3,227},{4,228},{5,229},{6,230},{7,231},{8... | collective-permute-start | bytes 1544 | tf_op jit(solution)/shard_map/ppermute | solution.py:23
  3.0 75.9 %collective-permute-start.9 = (bf16[128,3584]{1,0:T(8,128)(2,1)}, bf16[128,3584]{1,0:T(8,128)(2,1)S(1)}, u32[]{:S(2)}, u32[]{:S(2)}) collective-permute-start(bf16[128,3584]{1,0:T(8,128)(2,1)} %bitcast.82), channel_id=1, source_target_pairs={{0,224},{1,225},{2,226},{3,227},{4,228},{5,229},{6,230},{7,231},{8... | collective-permute-start | bytes 2752520 | tf_op jit(solution)/shard_map/ppermute | solution.py:23
  5.2 75.5 %collective-permute-start.10 = (bf16[256,3584]{1,0:T(8,128)(2,1)}, bf16[256,3584]{1,0:T(8,128)(2,1)}, u32[]{:S(2)}, u32[]{:S(2)}) collective-permute-start(bf16[256,3584]{1,0:T(8,128)(2,1)} %bitcast.78), channel_id=1, source_target_pairs={{0,2},{1,3},{2,0},{3,1},{4,6},{5,7},{6,4},{7,5},{8,10},{9,11},{10,... | collective-permute-start | bytes 5505032 | tf_op jit(solution)/shard_map/ppermute | solution.py:23
  12.7 10.3 %collective-permute-start.1 = (bf16[32,3584]{1,0:T(8,128)(2,1)}, bf16[32,3584]{1,0:T(8,128)(2,1)}, u32[]{:S(2)}, u32[]{:S(2)}) collective-permute-start(bf16[32,3584]{1,0:T(8,128)(2,1)} %get-tuple-element.44), channel_id=1, source_target_pairs={{0,0},{1,1},{2,2},{3,3},{4,4},{5,5},{6,6},{7,7},{8,8},{9,9},{10,10... | collective-permute-start | bytes 688136 | tf_op jit(solution)/shard_map/ppermute | solution.py:23
  16.7 17.1 %collective-permute-start.2 = (bf16[32,3584]{1,0:T(8,128)(2,1)}, bf16[32,3584]{1,0:T(8,128)(2,1)S(1)}, u32[]{:S(2)}, u32[]{:S(2)}) collective-permute-start(bf16[32,3584]{1,0:T(8,128)(2,1)} %get-tuple-element.43), channel_id=1, source_target_pairs={{0,4},{1,5},{2,6},{3,7},{4,8},{5,9},{6,10},{7,11},{8,12},{9,13},{1... | collective-permute-start | bytes 688136 | tf_op jit(solution)/shard_map/ppermute | solution.py:23
  18.7 29.8 %collective-permute-start.3 = (bf16[32,3584]{1,0:T(8,128)(2,1)S(1)}, bf16[32,3584]{1,0:T(8,128)(2,1)S(1)}, u32[]{:S(2)}, u32[]{:S(2)}) collective-permute-start(bf16[32,3584]{1,0:T(8,128)(2,1)S(1)} %get-tuple-element.42), channel_id=1, source_target_pairs={{0,8},{1,9},{2,10},{3,11},{4,12},{5,13},{6,14},{7,15},{8,16},{9,17... | collective-permute-start | bytes 688136 | tf_op jit(solution)/shard_map/ppermute | solution.py:23
  23.0 38.7 %collective-permute-start.4 = (bf16[32,3584]{1,0:T(8,128)(2,1)S(1)}, bf16[32,3584]{1,0:T(8,128)(2,1)S(1)}, u32[]{:S(2)}, u32[]{:S(2)}) collective-permute-start(bf16[32,3584]{1,0:T(8,128)(2,1)S(1)} %get-tuple-element.41), channel_id=1, source_target_pairs={{0,12},{1,13},{2,14},{3,15},{4,16},{5,17},{6,18},{7,19},{8,20},{9,... | collective-permute-start | bytes 688136 | tf_op jit(solution)/shard_map/ppermute | solution.py:23
  33.9 34.8 %collective-permute-start.5 = (bf16[32,3584]{1,0:T(8,128)(2,1)S(1)}, bf16[32,3584]{1,0:T(8,128)(2,1)S(1)}, u32[]{:S(2)}, u32[]{:S(2)}) collective-permute-start(bf16[32,3584]{1,0:T(8,128)(2,1)S(1)} %get-tuple-element.40), channel_id=1, source_target_pairs={{0,16},{1,17},{2,18},{3,19},{4,20},{5,21},{6,22},{7,23},{8,24},{9,... | collective-permute-start | bytes 688136 | tf_op jit(solution)/shard_map/ppermute | solution.py:23
  48.5 20.3 %collective-permute-start.6 = (bf16[32,3584]{1,0:T(8,128)(2,1)S(1)}, bf16[32,3584]{1,0:T(8,128)(2,1)S(1)}, u32[]{:S(2)}, u32[]{:S(2)}) collective-permute-start(bf16[32,3584]{1,0:T(8,128)(2,1)S(1)} %get-tuple-element.39), channel_id=1, source_target_pairs={{0,20},{1,21},{2,22},{3,23},{4,24},{5,25},{6,26},{7,27},{8,28},{9,... | collective-permute-start | bytes 688136 | tf_op jit(solution)/shard_map/ppermute | solution.py:23
  61.8 14.0 %collective-permute-start.7 = (bf16[32,3584]{1,0:T(8,128)(2,1)}, bf16[32,3584]{1,0:T(8,128)(2,1)S(1)}, u32[]{:S(2)}, u32[]{:S(2)}) collective-permute-start(bf16[32,3584]{1,0:T(8,128)(2,1)} %get-tuple-element.38), channel_id=1, source_target_pairs={{0,24},{1,25},{2,26},{3,27},{4,28},{5,29},{6,30},{7,31},{8,0},{9,1... | collective-permute-start | bytes 688136 | tf_op jit(solution)/shard_map/ppermute | solution.py:23
  68.6 8.9 %collective-permute-start.8 = (bf16[32,3584]{1,0:T(8,128)(2,1)}, bf16[32,3584]{1,0:T(8,128)(2,1)S(1)}, u32[]{:S(2)}, u32[]{:S(2)}) collective-permute-start(bf16[32,3584]{1,0:T(8,128)(2,1)} %get-tuple-element.37), channel_id=1, source_target_pairs={{0,28},{1,29},{2,30},{3,31},{4,0},{5,1},{6,2},{7,3},{8,4},{9,5},{1... | collective-permute-start | bytes 688136 | tf_op jit(solution)/shard_map/ppermute | solution.py:23
  68.8 11.9 %copy-start.4 = (bf16[16,32,512]{2,1,0:T(8,128)(2,1)S(1)}, bf16[16,32,512]{2,1,0:T(8,128)(2,1)}, u32[]{:S(2)}) copy-start(bf16[16,32,512]{2,1,0:T(8,128)(2,1)} %gather_fusion) | copy-start | bytes 1572868
  68.8 16.9 %copy-start.1 = (bf16[1,1,3584,256]{3,2,1,0:T(8,128)(2,1)S(1)}, bf16[1,1,3584,256]{3,2,1,0:T(8,128)(2,1)}, u32[]{:S(2)}) copy-start(bf16[1,1,3584,256]{3,2,1,0:T(8,128)(2,1)} %param.20) | copy-start | bytes 5505028
  80.7 2.0 collective-permute-start.12
  82.8 16.6 %collective-permute-start.13 = (bf16[3584,256]{1,0:T(8,128)(2,1)}, bf16[3584,256]{1,0:T(8,128)(2,1)}, u32[]{:S(2)}, u32[]{:S(2)}) collective-permute-start(bf16[3584,256]{1,0:T(8,128)(2,1)} %bitcast.5), channel_id=1, source_target_pairs={{0,1},{1,0},{2,3},{3,2},{4,5},{5,4},{6,7},{7,6},{8,9},{9,8},{10,11... | collective-permute-start | bytes 5505032 | tf_op jit(solution)/shard_map/ppermute | solution.py:23
  83.1 42.7 %collective-permute-start.11 = (bf16[256,3584]{1,0:T(8,128)(2,1)}, bf16[256,3584]{1,0:T(8,128)(2,1)}, u32[]{:S(2)}, u32[]{:S(2)}) collective-permute-start(bf16[256,3584]{1,0:T(8,128)(2,1)} %copy-done.7), channel_id=1, source_target_pairs={{0,34},{1,35},{2,32},{3,33},{4,38},{5,39},{6,36},{7,37},{8,42},{9,... | collective-permute-start | bytes 5505032 | tf_op jit(solution)/shard_map/ppermute | solution.py:23
  83.2 51.1 %collective-permute-start.16 = (bf16[256,3584]{1,0:T(8,128)(2,1)}, bf16[256,3584]{1,0:T(8,128)(2,1)}, u32[]{:S(2)}, u32[]{:S(2)}) collective-permute-start(bf16[256,3584]{1,0:T(8,128)(2,1)} %copy-done.7), channel_id=1, source_target_pairs={{0,32},{1,33},{2,34},{3,35},{4,36},{5,37},{6,38},{7,39},{8,40},{9,... | collective-permute-start | bytes 5505032 | tf_op jit(solution)/shard_map/ppermute | solution.py:23
  85.7 18.0 %collective-permute-start.14 = (bf16[3584,256]{1,0:T(8,128)(2,1)S(1)}, bf16[3584,256]{1,0:T(8,128)(2,1)}, u32[]{:S(2)}, u32[]{:S(2)}) collective-permute-start(bf16[3584,256]{1,0:T(8,128)(2,1)S(1)} %bitcast.61), channel_id=1, source_target_pairs={{0,1},{1,0},{2,3},{3,2},{4,5},{5,4},{6,7},{7,6},{8,9},{9,8},{10,11... | collective-permute-start | bytes 5505032 | tf_op jit(solution)/shard_map/ppermute | solution.py:23
  89.4 52.4 %collective-permute-start.19 = (bf16[256,3584]{1,0:T(8,128)(2,1)}, bf16[256,3584]{1,0:T(8,128)(2,1)}, u32[]{:S(2)}, u32[]{:S(2)}) collective-permute-start(bf16[256,3584]{1,0:T(8,128)(2,1)} %collective-permute-done.10), channel_id=1, source_target_pairs={{0,1},{1,0},{2,3},{3,2},{4,5},{5,4},{6,7},{7,6},{8,9},{9,8},{10,11... | collective-permute-start | bytes 5505032 | tf_op jit(solution)/shard_map/ppermute | solution.py:23
  89.9 53.4 %all-to-all-start.1 = ((bf16[8,32,3584]{2,1,0:T(8,128)(2,1)}), bf16[8,32,3584]{2,1,0:T(8,128)(2,1)}, u32[]{:S(2)}, u32[]{:S(2)}) async-start(bf16[8,32,3584]{2,1,0:T(8,128)(2,1)} %bitcast.25), calls=%async_computation.1 | async-start | bytes 3670016 | tf_op jit(solution)/shard_map/all_to_all | solution.py:74
  99.4 49.6 %collective-permute-start.18 = (bf16[256,3584]{1,0:T(8,128)(2,1)}, bf16[256,3584]{1,0:T(8,128)(2,1)}, u32[]{:S(2)}, u32[]{:S(2)}) collective-permute-start(bf16[256,3584]{1,0:T(8,128)(2,1)} %bitcast.79), channel_id=1, source_target_pairs={{0,1},{1,0},{2,3},{3,2},{4,5},{5,4},{6,7},{7,6},{8,9},{9,8},{10,11... | collective-permute-start | bytes 5505032 | tf_op jit(solution)/shard_map/ppermute | solution.py:23
  106.7 27.7 %copy-start.5 = (bf16[3584,1024]{1,0:T(8,128)(2,1)S(1)}, bf16[3584,1024]{1,0:T(8,128)(2,1)}, u32[]{:S(2)}) copy-start(bf16[3584,1024]{1,0:T(8,128)(2,1)} %constant_dynamic-update-slice_fusion.8) | copy-start | bytes 22020100
  131.7 9.4 %collective-permute-start.17 = (bf16[256,512]{1,0:T(8,128)(2,1)S(1)}, bf16[256,512]{1,0:T(8,128)(2,1)S(1)}, u32[]{:S(2)}, u32[]{:S(2)}) collective-permute-start(bf16[256,512]{1,0:T(8,128)(2,1)S(1)} %fusion.46), channel_id=1, source_target_pairs={{0,2},{1,3},{2,0},{3,1},{4,6},{5,7},{6,4},{7,5},{8,10},{9,11},{10,... | collective-permute-start | bytes 786440 | tf_op jit(solution)/shard_map/ppermute | solution.py:23
  148.0 13.7 %collective-permute-start.20 = (bf16[256,512]{1,0:T(8,128)(2,1)}, bf16[256,512]{1,0:T(8,128)(2,1)}, u32[]{:S(2)}, u32[]{:S(2)}) collective-permute-start(bf16[256,512]{1,0:T(8,128)(2,1)} %fusion.22), channel_id=1, source_target_pairs={{0,2},{1,3},{2,0},{3,1},{4,6},{5,7},{6,4},{7,5},{8,10},{9,11},{10,... | collective-permute-start | bytes 786440 | tf_op jit(solution)/shard_map/ppermute | solution.py:23
  154.0 64.5 %all-to-all-start = ((bf16[8,32,3584]{2,1,0:T(8,128)(2,1)}), bf16[8,32,3584]{2,1,0:T(8,128)(2,1)S(1)}, u32[]{:S(2)}, u32[]{:S(2)}) async-start(bf16[8,32,3584]{2,1,0:T(8,128)(2,1)} %bitcast.63), calls=%async_computation | async-start | bytes 3670016 | tf_op jit(solution)/shard_map/all_to_all | solution.py:74
  166.0 48.9 %slice-start = ((s8[7340032]{0:T(1024)(128)(4,1)}), s8[4194304]{0:T(1024)(128)(4,1)S(1)}, s32[]{:S(2)}) async-start(s8[7340032]{0:T(1024)(128)(4,1)} %bitcast.68), calls=%async_computation.3 | async-start | bytes 8388608
  167.5 47.5 %slice-start.1 = ((s8[7340032]{0:T(1024)(128)(4,1)}), s8[3145728]{0:T(1024)(128)(4,1)S(1)}, s32[]{:S(2)}) async-start(s8[7340032]{0:T(1024)(128)(4,1)} %bitcast.68), calls=%async_computation.4 | async-start | bytes 6291456
  172.9 42.1 %collective-permute-start.21 = (bf16[256,3584]{1,0:T(8,128)(2,1)S(1)}, bf16[256,3584]{1,0:T(8,128)(2,1)S(1)}, u32[]{:S(2)}, u32[]{:S(2)}) collective-permute-start(bf16[256,3584]{1,0:T(8,128)(2,1)S(1)} %convolution_convert_fusion), channel_id=1, source_target_pairs={{0,2},{1,3},{2,0},{3,1},{4,6},{5,7},{6,4},{7,5},{8,10},{9,11},{10,... | collective-permute-start | bytes 5505032 | tf_op jit(solution)/shard_map/ppermute | solution.py:23
  174.1 40.6 %collective-permute-start.22 = (f32[256]{0:T(256)S(1)}, f32[256]{0:T(256)S(1)}, u32[]{:S(2)}, u32[]{:S(2)}) collective-permute-start(f32[256]{0:T(256)S(1)} %get-tuple-element.35), channel_id=1, source_target_pairs={{0,2},{1,3},{2,0},{3,1},{4,6},{5,7},{6,4},{7,5},{8,10},{9,11},{10,... | collective-permute-start | bytes 3080 | tf_op jit(solution)/shard_map/ppermute | solution.py:23
  218.5 27.3 %copy-start.10 = (f32[1,128]{1,0:T(1,128)S(1)}, f32[1,128]{1,0:T(1,128)}, u32[]{:S(2)}) copy-start(f32[1,128]{1,0:T(1,128)} %param.13) | copy-start | bytes 1540
  219.7 50.9 %all-to-all-start.2 = ((bf16[8,32,3712]{2,1,0:T(8,128)(2,1)}), bf16[8,32,3712]{2,1,0:T(8,128)(2,1)S(1)}, u32[]{:S(2)}, u32[]{:S(2)}) async-start(bf16[8,32,3712]{2,1,0:T(8,128)(2,1)} %bitcast.27), calls=%async_computation.2 | async-start | bytes 3801088 | tf_op jit(solution)/shard_map/all_to_all | solution.py:74
  226.7 19.1 %collective-permute-start.15 = (bf16[128,3584]{1,0:T(8,128)(2,1)}, bf16[128,3584]{1,0:T(8,128)(2,1)}, u32[]{:S(2)}, u32[]{:S(2)}) collective-permute-start(bf16[128,3584]{1,0:T(8,128)(2,1)} %bitcast.64), channel_id=1, source_target_pairs={{0,32},{1,33},{2,34},{3,35},{4,36},{5,37},{6,38},{7,39},{8,40},{9,... | collective-permute-start | bytes 2752520 | tf_op jit(solution)/shard_map/ppermute | solution.py:23
  (9 other events, 47.3 us)
where the time goes:
time: 274 us; the launch traced here: 273 us
  waiting for transfers between devices  137 us (50%)
  starting transfers between devices  68.6 us (25%)
  matrix products  36.7 us (13%)
  local copies, waits for them, and re-layouts  20.1 us (7%)
  other arithmetic  9.5 us (3%)
    ppermute x23, waiting for transfers between devices, send(): return lax.ppermute(value, AXES, pairs)  114 us
    ppermute x23, starting transfers between devices, send(): return lax.ppermute(value, AXES, pairs)  46.3 us
    all_to_all x3, waiting for transfers between devices, exchange(): lax.all_to_all(rows, 'expert', 0, 0, axis_index_groups=groups, tiled=True)  23.3 us
    all_to_all x3, starting transfers between devices, exchange(): lax.all_to_all(rows, 'expert', 0, 0, axis_index_groups=groups, tiled=True)  22.2 us
    dot_general x7, matrix products, dot(): return jnp.dot(a, b, preferred_element_type=jnp.float32)  20.2 us
    dot_general x4, matrix products, dot_last(): lax.dot_general(a, b, (((1,), (1,)), ((), ())), preferred_element_type=jn...  16.4 us
    unnamed x40, local copies, waits for them, and re-layouts  10.9 us
  transfers between devices with their start and end apart: 26, of which 12 were waited for; matrix products, arithmetic and copies ran while one was open for 22% of the time, Pallas kernels for 0%

commit v1 on v0

--- a/solution.py
+++ b/solution.py
@@ -105,6 +105,9 @@
     packed = pack(forward_input[0], onward_keys, slots)
     order = [distance for pair in zip(range(planes // 2, planes), range(planes // 2 - 1, -1, -1)) for distance in pair]
     arrived = {d: onward(packed[d * capacity:(d + 1) * capacity], d) for d in order}
+    backward_packed, arrived[order[2]] = lax.optimization_barrier(
+        (pack(upstream, backward_keys, slots), arrived[order[2]])
+    )
     forward_rows = jnp.concatenate([arrived[d] for d in range(planes)], axis=0)
 
     turns = jnp.arange(planes, dtype=jnp.int32) * WS
@@ -114,7 +117,7 @@
     saved_own, saved_next = saved[mine].reshape(2 * slots, -1), saved[other].reshape(2 * slots, -1)
 
     down_far = swap_half(down_own)
-    backward_packed = pack(upstream, backward_keys, slots)
+    gate_first, up_first = gate_own, up_own
     forward_rows, backward_packed, down_far, gate_own, up_own, saved_next, saved_own, forward_first = lax.optimization_barrier(
         (forward_rows, backward_packed, down_far, gate_own, up_own, saved_next, saved_own, forward_input[0])
     )
@@ -125,7 +128,7 @@
         (saved_next, backward_packed, gate_own, up_own, down_own, down_far)
     )
     backward_rows = exchange(backward_packed, planes)
-    gates = jnp.concatenate([gate_own, swap_core(gate_own), up_own, swap_core(up_own)], axis=1)
+    gates = jnp.concatenate([gate_first, swap_core(gate_own), up_first, swap_core(up_own)], axis=1)
     down = jnp.concatenate([down_own, swap_core(down_own), down_far, swap_core(down_far)], axis=0)
     near = down.shape[0] // 2
     units = near // 2
@@ -149,7 +152,6 @@
     forward_output = (inputs.astype(jnp.float32) + forward_weight[0][:, None] * mixed).astype(jnp.bfloat16)
 
     back_far = swap_half(dot_last(backward_rows, down[near:]).astype(jnp.bfloat16))
-    back_near = dot_last(backward_rows, down[:near])
 
     def back_of(back_r, gate, upper):
         gate, upper = gate.astype(jnp.float32), upper.astype(jnp.float32)
@@ -159,12 +161,15 @@
         share = jnp.sum(back_r * saved_hidden, axis=1)
         d_gate = (back_r * upper * sigma * (1.0 + gate * (1.0 - sigma))).astype(jnp.bfloat16)
         d_up = (back_r * active).astype(jnp.bfloat16)
-        return dot_last(jnp.concatenate([d_gate, d_up], axis=1), gates), share
-
-    far_part, far_share = back_of(back_far.astype(jnp.float32), g[slots:], u[slots:])
+        return jnp.concatenate([d_gate, d_up], axis=1), share
+
+    far_terms, far_share = back_of(back_far.astype(jnp.float32), g[slots:], u[slots:])
+    far_terms, backward_rows = lax.optimization_barrier((far_terms, backward_rows))
+    far_part = dot_last(far_terms, gates)
     far_part = swap_half(far_part.astype(jnp.bfloat16))
     far_share = swap_half(far_share)
-    near_part, near_share = back_of(back_near, g[:slots], u[:slots])
+    near_terms, near_share = back_of(dot_last(backward_rows, down[:near]), g[:slots], u[:slots])
+    near_part = dot_last(near_terms, gates)
     part = (near_part + far_part.astype(jnp.float32)).astype(jnp.bfloat16)
     rest, terms = near_share + far_share, []
     for _ in range(3):

time: 274 us -> 263 us (0.960)
  waiting for transfers between devices: 137 us -> 126 us
  local copies, waits for them, and re-layouts: 20.1 us -> 11.6 us
  starting transfers between devices: 68.6 us -> 76.5 us
  other arithmetic: 9.5 us -> 13.5 us
  matrix products: 36.7 us -> 33.9 us
    ppermute x23, starting transfers between devices: 46.3 us -> 59 us  [send(): return lax.ppermute(value, AXES, pairs)]
    ppermute x23, waiting for transfers between devices: 114 us -> 104 us  [send(): return lax.ppermute(value, AXES, pairs)]
    all_to_all x3, starting transfers between devices: 22.2 us -> 17.5 us  [exchange(): lax.all_to_all(rows, 'expert', 0, 0, axis_index_groups=groups, tiled=True)]
    concatenate x0 -> x2, other arithmetic: none -> 4.14 us  [the longest x1 4.09 us: per_device(): jnp.concatenate([gate_first, swap_core(gate_own), up_first, swap_core(up_...]
    unnamed x40 -> x31, local copies, waits for them, and re-layouts: 10.9 us -> 7.1 us
    concatenate x1 -> x0, local copies, waits for them, and re-layouts: 2.93 us -> none  [per_device(): jnp.concatenate([gate_own, swap_core(gate_own), up_own, swap_core(up_own)...]
  transfers between devices with their start and end apart: 26 -> 26, of which waited for: 12 -> 12; matrix products, arithmetic and copies ran while one was open for 22% -> 21% of each run, Pallas kernels for 0% -> 0%
where the time goes in v1:
time: 263 us; the launch traced here: 262 us
  waiting for transfers between devices  126 us (48%)
  starting transfers between devices  76.5 us (29%)
  matrix products  33.9 us (13%)
  other arithmetic  13.5 us (5%)
  local copies, waits for them, and re-layouts  11.6 us (4%)
    ppermute x23, waiting for transfers between devices, send(): return lax.ppermute(value, AXES, pairs)  104 us
    ppermute x23, starting transfers between devices, send(): return lax.ppermute(value, AXES, pairs)  59 us
    all_to_all x3, waiting for transfers between devices, exchange(): lax.all_to_all(rows, 'expert', 0, 0, axis_index_groups=groups, tiled=True)  21.8 us
    dot_general x7, matrix products, dot(): return jnp.dot(a, b, preferred_element_type=jnp.float32)  18.1 us
    all_to_all x3, starting transfers between devices, exchange(): lax.all_to_all(rows, 'expert', 0, 0, axis_index_groups=groups, tiled=True)  17.5 us
    dot_general x4, matrix products, dot_last(): lax.dot_general(a, b, (((1,), (1,)), ((), ())), preferred_element_type=jn...  15.8 us
    unnamed x31, local copies, waits for them, and re-layouts  7.1 us
  transfers between devices with their start and end apart: 26, of which 12 were waited for; matrix products, arithmetic and copies ran while one was open for 21% of the time, Pallas kernels for 0%

profile of v1, /device:TPU:2, one launch (start us, length us, event | category | flops | bytes accessed | tf_op | source)
XLA Modules:
  0.0 262.2 jit_solution(12452497173313205027)
XLA Ops:
  0.6 2.3 collective-permute-start
  3.0 2.2 collective-permute-start.6
  5.2 2.1 collective-permute-start.10
  18.1 4.3 %collective-permute-start.3 = (bf16[32,3584]{1,0:T(8,128)(2,1)}, bf16[32,3584]{1,0:T(8,128)(2,1)S(1)}, u32[]{:S(2)}, u32[]{:S(2)}) collective-permute-start(bf16[32,3584]{1,0:T(8,128)(2,1)} %get-tuple-element.50), channel_id=1, source_target_pairs={{0,8},{1,9},{2,10},{3,11},{4,12},{5,13},{6,14},{7,15},{8,16},{9,17... | collective-permute-start | bytes 688136 | tf_op jit(solution)/shard_map/ppermute | solution.py:23
  22.8 8.4 %collective-permute-start.4 = (bf16[32,3584]{1,0:T(8,128)(2,1)}, bf16[32,3584]{1,0:T(8,128)(2,1)S(1)}, u32[]{:S(2)}, u32[]{:S(2)}) collective-permute-start(bf16[32,3584]{1,0:T(8,128)(2,1)} %get-tuple-element.49), channel_id=1, source_target_pairs={{0,12},{1,13},{2,14},{3,15},{4,16},{5,17},{6,18},{7,19},{8,20},{9,... | collective-permute-start | bytes 688136 | tf_op jit(solution)/shard_map/ppermute | solution.py:23
  33.2 5.6 %collective-permute-start.5 = (bf16[32,3584]{1,0:T(8,128)(2,1)}, bf16[32,3584]{1,0:T(8,128)(2,1)S(1)}, u32[]{:S(2)}, u32[]{:S(2)}) collective-permute-start(bf16[32,3584]{1,0:T(8,128)(2,1)} %get-tuple-element.48), channel_id=1, source_target_pairs={{0,16},{1,17},{2,18},{3,19},{4,20},{5,21},{6,22},{7,23},{8,24},{9,... | collective-permute-start | bytes 688136 | tf_op jit(solution)/shard_map/ppermute | solution.py:23
  39.5 8.8 %collective-permute-done.3 = bf16[32,3584]{1,0:T(8,128)(2,1)S(1)} collective-permute-done((bf16[32,3584]{1,0:T(8,128)(2,1)}, bf16[32,3584]{1,0:T(8,128)(2,1)S(1)}, u32[]{:S(2)}, u32[]{:S(2)}) %collective-permute-start.3) | collective-permute-done | bytes 229408 | tf_op jit(solution)/shard_map/ppermute | solution.py:23
  48.3 3.5 %collective-permute-start.7 = (bf16[32,3584]{1,0:T(8,128)(2,1)}, bf16[32,3584]{1,0:T(8,128)(2,1)S(1)}, u32[]{:S(2)}, u32[]{:S(2)}) collective-permute-start(bf16[32,3584]{1,0:T(8,128)(2,1)} %get-tuple-element.47), channel_id=1, source_target_pairs={{0,20},{1,21},{2,22},{3,23},{4,24},{5,25},{6,26},{7,27},{8,28},{9,... | collective-permute-start | bytes 688136 | tf_op jit(solution)/shard_map/ppermute | solution.py:23
  52.5 3.1 %collective-permute-done.4 = bf16[32,3584]{1,0:T(8,128)(2,1)S(1)} collective-permute-done((bf16[32,3584]{1,0:T(8,128)(2,1)}, bf16[32,3584]{1,0:T(8,128)(2,1)S(1)}, u32[]{:S(2)}, u32[]{:S(2)}) %collective-permute-start.4) | collective-permute-done | bytes 229408 | tf_op jit(solution)/shard_map/ppermute | solution.py:23
  55.7 13.4 %collective-permute-start.8 = (bf16[32,3584]{1,0:T(8,128)(2,1)S(1)}, bf16[32,3584]{1,0:T(8,128)(2,1)S(1)}, u32[]{:S(2)}, u32[]{:S(2)}) collective-permute-start(bf16[32,3584]{1,0:T(8,128)(2,1)S(1)} %get-tuple-element.46), channel_id=1, source_target_pairs={{0,24},{1,25},{2,26},{3,27},{4,28},{5,29},{6,30},{7,31},{8,0},{9,1... | collective-permute-start | bytes 688136 | tf_op jit(solution)/shard_map/ppermute | solution.py:23
  75.7 3.5 %collective-permute-done.9 = bf16[32,3584]{1,0:T(8,128)(2,1)S(1)} collective-permute-done((bf16[32,3584]{1,0:T(8,128)(2,1)S(1)}, bf16[32,3584]{1,0:T(8,128)(2,1)S(1)}, u32[]{:S(2)}, u32[]{:S(2)}) %collective-permute-start.9) | collective-permute-done | bytes 229408 | tf_op jit(solution)/shard_map/ppermute | solution.py:23
  82.6 2.9 %collective-permute-start.16 = (bf16[256,3584]{1,0:T(8,128)(2,1)}, bf16[256,3584]{1,0:T(8,128)(2,1)}, u32[]{:S(2)}, u32[]{:S(2)}) collective-permute-start(bf16[256,3584]{1,0:T(8,128)(2,1)} %constant_dynamic-update-slice_fusion), channel_id=1, source_target_pairs={{0,32},{1,33},{2,34},{3,35},{4,36},{5,37},{6,38},{7,39},{8,40},{9,... | collective-permute-start | bytes 5505032 | tf_op jit(solution)/shard_map/ppermute | solution.py:23
  85.6 5.3 %all-to-all-start.1 = ((bf16[8,32,3584]{2,1,0:T(8,128)(2,1)}), bf16[8,32,3584]{2,1,0:T(8,128)(2,1)}, u32[]{:S(2)}, u32[]{:S(2)}) async-start(bf16[8,32,3584]{2,1,0:T(8,128)(2,1)} %bitcast.25), calls=%async_computation.1 | async-start | bytes 3670016 | tf_op jit(solution)/shard_map/all_to_all | solution.py:74
  91.8 4.1 %pad_maximum_fusion = bf16[3584,1024]{1,0:T(8,128)(2,1)S(1)} fusion(bf16[3584,256]{1,0:T(8,128)(2,1)} %collective-permute-done.14, bf16[3584,256]{1,0:T(8,128)(2,1)} %bitcast.6, bf16[3584,256]{1,0:T(8,128)(2,1)} %collective-permute-done.13, bf16[3584,256]{1,0:T(8,128)(2,1)} %bitcast.5), kind=kLoop, calls=%fused_computation.3 | loop fusion | flops 29360128 | bytes 14680064 | tf_op jit(solution)/shard_map/concatenate | solution.py:131
  95.9 28.8 %collective-permute-done.11 = bf16[256,3584]{1,0:T(8,128)(2,1)} collective-permute-done((bf16[256,3584]{1,0:T(8,128)(2,1)}, bf16[256,3584]{1,0:T(8,128)(2,1)}, u32[]{:S(2)}, u32[]{:S(2)}) %collective-permute-start.11) | collective-permute-done | bytes 1835040 | tf_op jit(solution)/shard_map/ppermute | solution.py:23
  124.7 3.6 %fusion.77 = f32[256,1024]{1,0:T(8,128)S(1)} fusion(bf16[256,3584]{1,0:T(8,128)(2,1)} %collective-permute-done.11, bf16[3584,1024]{1,0:T(8,128)(2,1)S(1)} %pad_maximum_fusion), kind=kOutput, calls=%fused_computation.162 | convolution fusion | flops 1879048192 | bytes 10223616 | tf_op jit(solution)/shard_map/dot_general | solution.py:47
  128.4 2.8 %collective-permute-start.17 = (bf16[256,512]{1,0:T(8,128)(2,1)S(1)}, bf16[256,512]{1,0:T(8,128)(2,1)S(1)}, u32[]{:S(2)}, u32[]{:S(2)}) collective-permute-start(bf16[256,512]{1,0:T(8,128)(2,1)S(1)} %fusion.46), channel_id=1, source_target_pairs={{0,2},{1,3},{2,0},{3,1},{4,6},{5,7},{6,4},{7,5},{8,10},{9,11},{10,... | collective-permute-start | bytes 786440 | tf_op jit(solution)/shard_map/ppermute | solution.py:23
  131.2 3.6 %fusion.78 = f32[256,1024]{1,0:T(8,128)S(1)} fusion(bf16[256,3584]{1,0:T(8,128)(2,1)} %collective-permute-done.16, bf16[3584,1024]{1,0:T(8,128)(2,1)S(1)} %pad_maximum_fusion), kind=kOutput, calls=%fused_computation.163 | convolution fusion | flops 1879048192 | bytes 10223616 | tf_op jit(solution)/shard_map/dot_general | solution.py:47
  134.9 2.6 collective-permute-done.17
  138.4 4.6 %fusion.22 = bf16[256,512]{1,0:T(8,128)(2,1)} fusion(bf16[256,3584]{1,0:T(8,128)(2,1)} %bitcast.26, bf16[256,3584]{1,0:T(8,128)(2,1)} %collective-permute-done.19, bf16[256,3584]{1,0:T(8,128)(2,1)} %collective-permute-done.10), kind=kOutput, calls=%fused_computation.32 | convolution fusion | flops 946995200 | bytes 5767168 | tf_op jit(solution)/shard_map/dot_general | solution.py:51
  143.0 2.7 %collective-permute-start.20 = (bf16[256,512]{1,0:T(8,128)(2,1)}, bf16[256,512]{1,0:T(8,128)(2,1)}, u32[]{:S(2)}, u32[]{:S(2)}) collective-permute-start(bf16[256,512]{1,0:T(8,128)(2,1)} %fusion.22), channel_id=1, source_target_pairs={{0,2},{1,3},{2,0},{3,1},{4,6},{5,7},{6,4},{7,5},{8,10},{9,11},{10,... | collective-permute-start | bytes 786440 | tf_op jit(solution)/shard_map/ppermute | solution.py:23
  145.6 5.0 %fusion.8 = bf16[256,3584]{1,0:T(8,128)(2,1)} fusion(bf16[256,1024]{1,0:T(8,128)(2,1)S(1)} %bitcast_select_fusion, bf16[256,3584]{1,0:T(8,128)(2,1)} %collective-permute-done.19, bf16[256,3584]{1,0:T(8,128)(2,1)} %collective-permute-done.10, bf16[256,3584]{1,0:T(8,128)(2,1)} %collective-permute-done.18, bf16[256,3584]{1,0:T(8,128)(2,1)S(1)} %bitcast.79), kind=kOutput, calls=%fused_computation.13 | convolution fusion | flops 1909325824 | bytes 9699328 | tf_op jit(solution)/shard_map/dot_general | solution.py:47
  150.6 5.3 %all-to-all-start = ((bf16[8,32,3584]{2,1,0:T(8,128)(2,1)}), bf16[8,32,3584]{2,1,0:T(8,128)(2,1)S(1)}, u32[]{:S(2)}, u32[]{:S(2)}) async-start(bf16[8,32,3584]{2,1,0:T(8,128)(2,1)} %bitcast.64), calls=%async_computation | async-start | bytes 3670016 | tf_op jit(solution)/shard_map/all_to_all | solution.py:74
  157.2 5.4 %convolution_convert_fusion = bf16[256,3584]{1,0:T(8,128)(2,1)S(1)} fusion(bf16[256,1024]{1,0:T(8,128)(2,1)S(1)} %pad_maximum_fusion.4, bf16[3584,1024]{1,0:T(8,128)(2,1)} %copy-done), kind=kOutput, calls=%fused_computation.14 | convolution fusion | flops 1879965696 | bytes 9699328 | tf_op jit(solution)/shard_map/dot_general | solution.py:51
  163.9 3.8 %fusion.36 = (f32[256]{0:T(256)S(1)}, f32[256]{0:T(256)S(1)}, bf16[256,512]{1,0:T(8,128)(2,1)S(1)}, bf16[256,512]{1,0:T(8,128)(2,1)S(1)}) fusion(bf16[256,512]{1,0:T(8,128)(2,1)} %collective-permute-done.20, bf16[512,256]{1,0:T(8,128)(2,1)S(1)} %copy-done.2, bf16[512,256]{1,0:T(8,128)(2,1)S(1)} %get-tuple-element.58, ...), kind=kOutput, calls=%fused_computation.57 | convolution fusion | flops 952630784 | bytes 7342080 | tf_op jit(solution)/shard_map/dot_general | solution.py:51
  167.6 2.7 %collective-permute-start.22 = (f32[256]{0:T(256)S(1)}, f32[256]{0:T(256)S(1)}, u32[]{:S(2)}, u32[]{:S(2)}) collective-permute-start(f32[256]{0:T(256)S(1)} %get-tuple-element.43), channel_id=1, source_target_pairs={{0,2},{1,3},{2,0},{3,1},{4,6},{5,7},{6,4},{7,5},{8,10},{9,11},{10,... | collective-permute-start | bytes 3080 | tf_op jit(solution)/shard_map/ppermute | solution.py:23
  170.3 33.9 %collective-permute-done.22 = f32[256]{0:T(256)S(1)} collective-permute-done((f32[256]{0:T(256)S(1)}, f32[256]{0:T(256)S(1)}, u32[]{:S(2)}, u32[]{:S(2)}) %collective-permute-start.22) | collective-permute-done | bytes 1056 | tf_op jit(solution)/shard_map/ppermute | solution.py:23
  204.5 2.1 fusion.11
  209.2 6.9 %all-to-all-start.2 = ((bf16[8,32,3712]{2,1,0:T(8,128)(2,1)}), bf16[8,32,3712]{2,1,0:T(8,128)(2,1)S(1)}, u32[]{:S(2)}, u32[]{:S(2)}) async-start(bf16[8,32,3712]{2,1,0:T(8,128)(2,1)} %bitcast.27), calls=%async_computation.2 | async-start | bytes 3801088 | tf_op jit(solution)/shard_map/all_to_all | solution.py:74
  216.6 18.4 %collective-permute-done.15 = bf16[128,3584]{1,0:T(8,128)(2,1)} collective-permute-done((bf16[128,3584]{1,0:T(8,128)(2,1)}, bf16[128,3584]{1,0:T(8,128)(2,1)}, u32[]{:S(2)}, u32[]{:S(2)}) %collective-permute-start.15) | collective-permute-done | bytes 917536 | tf_op jit(solution)/shard_map/ppermute | solution.py:23
  235.0 3.1 %fusion.25 = bf16[1,128,3584]{2,1,0:T(8,128)(2,1)} fusion(bf16[128,3584]{1,0:T(8,128)(2,1)} %collective-permute-done.15, bf16[256,3584]{1,0:T(8,128)(2,1)} %bitcast.61, f32[128]{0:T(128)S(1)} %bitcast.74, s32[128]{0:T(128)S(1)} %multiply_add_fusion), kind=kOutput, calls=%fused_computation.34 | convolution fusion | flops 236748800 | bytes 3671040 | tf_op jit(solution)/shard_map/dot_general | solution.py:47
  238.1 21.8 %all-to-all-done.2 = bf16[8,32,3712]{2,1,0:T(8,128)(2,1)S(1)} async-done(((bf16[8,32,3712]{2,1,0:T(8,128)(2,1)}), bf16[8,32,3712]{2,1,0:T(8,128)(2,1)S(1)}, u32[]{:S(2)}, u32[]{:S(2)}) %all-to-all-start.2) | async-done | bytes 1900576 | tf_op jit(solution)/shard_map/all_to_all | solution.py:74
  (109 shorter events, 34.8 us)
Async XLA Ops:
  0.6 10.4 %copy-start.3 = (bf16[1,128,3584]{2,1,0:T(8,128)(2,1)S(1)}, bf16[1,128,3584]{2,1,0:T(8,128)(2,1)}, u32[]{:S(2)}) copy-start(bf16[1,128,3584]{2,1,0:T(8,128)(2,1)} %param.11) | copy-start | bytes 2752516
  0.6 9.9 %collective-permute-start = (s32[128]{0:T(128)}, s32[128]{0:T(128)S(1)}, u32[]{:S(2)}, u32[]{:S(2)}) collective-permute-start(s32[128]{0:T(128)} %bitcast.71), channel_id=1, source_target_pairs={{0,224},{1,225},{2,226},{3,227},{4,228},{5,229},{6,230},{7,231},{8... | collective-permute-start | bytes 1544 | tf_op jit(solution)/shard_map/ppermute | solution.py:23
  3.0 67.4 %collective-permute-start.6 = (bf16[128,3584]{1,0:T(8,128)(2,1)}, bf16[128,3584]{1,0:T(8,128)(2,1)S(1)}, u32[]{:S(2)}, u32[]{:S(2)}) collective-permute-start(bf16[128,3584]{1,0:T(8,128)(2,1)} %bitcast.81), channel_id=1, source_target_pairs={{0,224},{1,225},{2,226},{3,227},{4,228},{5,229},{6,230},{7,231},{8... | collective-permute-start | bytes 2752520 | tf_op jit(solution)/shard_map/ppermute | solution.py:23
  5.2 74.7 %collective-permute-start.10 = (bf16[256,3584]{1,0:T(8,128)(2,1)}, bf16[256,3584]{1,0:T(8,128)(2,1)}, u32[]{:S(2)}, u32[]{:S(2)}) collective-permute-start(bf16[256,3584]{1,0:T(8,128)(2,1)} %bitcast.77), channel_id=1, source_target_pairs={{0,2},{1,3},{2,0},{3,1},{4,6},{5,7},{6,4},{7,5},{8,10},{9,11},{10,... | collective-permute-start | bytes 5505032 | tf_op jit(solution)/shard_map/ppermute | solution.py:23
  12.8 10.0 %collective-permute-start.1 = (bf16[32,3584]{1,0:T(8,128)(2,1)}, bf16[32,3584]{1,0:T(8,128)(2,1)}, u32[]{:S(2)}, u32[]{:S(2)}) collective-permute-start(bf16[32,3584]{1,0:T(8,128)(2,1)} %get-tuple-element.52), channel_id=1, source_target_pairs={{0,0},{1,1},{2,2},{3,3},{4,4},{5,5},{6,6},{7,7},{8,8},{9,9},{10,10... | collective-permute-start | bytes 688136 | tf_op jit(solution)/shard_map/ppermute | solution.py:23
  16.1 17.1 %collective-permute-start.2 = (bf16[32,3584]{1,0:T(8,128)(2,1)}, bf16[32,3584]{1,0:T(8,128)(2,1)S(1)}, u32[]{:S(2)}, u32[]{:S(2)}) collective-permute-start(bf16[32,3584]{1,0:T(8,128)(2,1)} %get-tuple-element.51), channel_id=1, source_target_pairs={{0,4},{1,5},{2,6},{3,7},{4,8},{5,9},{6,10},{7,11},{8,12},{9,13},{1... | collective-permute-start | bytes 688136 | tf_op jit(solution)/shard_map/ppermute | solution.py:23
  18.1 30.2 %collective-permute-start.3 = (bf16[32,3584]{1,0:T(8,128)(2,1)}, bf16[32,3584]{1,0:T(8,128)(2,1)S(1)}, u32[]{:S(2)}, u32[]{:S(2)}) collective-permute-start(bf16[32,3584]{1,0:T(8,128)(2,1)} %get-tuple-element.50), channel_id=1, source_target_pairs={{0,8},{1,9},{2,10},{3,11},{4,12},{5,13},{6,14},{7,15},{8,16},{9,17... | collective-permute-start | bytes 688136 | tf_op jit(solution)/shard_map/ppermute | solution.py:23
  22.8 32.8 %collective-permute-start.4 = (bf16[32,3584]{1,0:T(8,128)(2,1)}, bf16[32,3584]{1,0:T(8,128)(2,1)S(1)}, u32[]{:S(2)}, u32[]{:S(2)}) collective-permute-start(bf16[32,3584]{1,0:T(8,128)(2,1)} %get-tuple-element.49), channel_id=1, source_target_pairs={{0,12},{1,13},{2,14},{3,15},{4,16},{5,17},{6,18},{7,19},{8,20},{9,... | collective-permute-start | bytes 688136 | tf_op jit(solution)/shard_map/ppermute | solution.py:23
  33.2 36.5 %collective-permute-start.5 = (bf16[32,3584]{1,0:T(8,128)(2,1)}, bf16[32,3584]{1,0:T(8,128)(2,1)S(1)}, u32[]{:S(2)}, u32[]{:S(2)}) collective-permute-start(bf16[32,3584]{1,0:T(8,128)(2,1)} %get-tuple-element.48), channel_id=1, source_target_pairs={{0,16},{1,17},{2,18},{3,19},{4,20},{5,21},{6,22},{7,23},{8,24},{9,... | collective-permute-start | bytes 688136 | tf_op jit(solution)/shard_map/ppermute | solution.py:23
  48.3 24.0 %collective-permute-start.7 = (bf16[32,3584]{1,0:T(8,128)(2,1)}, bf16[32,3584]{1,0:T(8,128)(2,1)S(1)}, u32[]{:S(2)}, u32[]{:S(2)}) collective-permute-start(bf16[32,3584]{1,0:T(8,128)(2,1)} %get-tuple-element.47), channel_id=1, source_target_pairs={{0,20},{1,21},{2,22},{3,23},{4,24},{5,25},{6,26},{7,27},{8,28},{9,... | collective-permute-start | bytes 688136 | tf_op jit(solution)/shard_map/ppermute | solution.py:23
  55.7 19.4 %collective-permute-start.8 = (bf16[32,3584]{1,0:T(8,128)(2,1)S(1)}, bf16[32,3584]{1,0:T(8,128)(2,1)S(1)}, u32[]{:S(2)}, u32[]{:S(2)}) collective-permute-start(bf16[32,3584]{1,0:T(8,128)(2,1)S(1)} %get-tuple-element.46), channel_id=1, source_target_pairs={{0,24},{1,25},{2,26},{3,27},{4,28},{5,29},{6,30},{7,31},{8,0},{9,1... | collective-permute-start | bytes 688136 | tf_op jit(solution)/shard_map/ppermute | solution.py:23
  69.7 9.5 %collective-permute-start.9 = (bf16[32,3584]{1,0:T(8,128)(2,1)S(1)}, bf16[32,3584]{1,0:T(8,128)(2,1)S(1)}, u32[]{:S(2)}, u32[]{:S(2)}) collective-permute-start(bf16[32,3584]{1,0:T(8,128)(2,1)S(1)} %get-tuple-element.45), channel_id=1, source_target_pairs={{0,28},{1,29},{2,30},{3,31},{4,0},{5,1},{6,2},{7,3},{8,4},{9,5},{1... | collective-permute-start | bytes 688136 | tf_op jit(solution)/shard_map/ppermute | solution.py:23
  79.9 1.9 collective-permute-start.12
  81.8 9.8 %collective-permute-start.13 = (bf16[3584,256]{1,0:T(8,128)(2,1)}, bf16[3584,256]{1,0:T(8,128)(2,1)}, u32[]{:S(2)}, u32[]{:S(2)}) collective-permute-start(bf16[3584,256]{1,0:T(8,128)(2,1)} %bitcast.5), channel_id=1, source_target_pairs={{0,1},{1,0},{2,3},{3,2},{4,5},{5,4},{6,7},{7,6},{8,9},{9,8},{10,11... | collective-permute-start | bytes 5505032 | tf_op jit(solution)/shard_map/ppermute | solution.py:23
  82.0 9.9 %collective-permute-start.14 = (bf16[3584,256]{1,0:T(8,128)(2,1)}, bf16[3584,256]{1,0:T(8,128)(2,1)}, u32[]{:S(2)}, u32[]{:S(2)}) collective-permute-start(bf16[3584,256]{1,0:T(8,128)(2,1)} %bitcast.6), channel_id=1, source_target_pairs={{0,1},{1,0},{2,3},{3,2},{4,5},{5,4},{6,7},{7,6},{8,9},{9,8},{10,11... | collective-permute-start | bytes 5505032 | tf_op jit(solution)/shard_map/ppermute | solution.py:23
  82.3 42.4 %collective-permute-start.11 = (bf16[256,3584]{1,0:T(8,128)(2,1)}, bf16[256,3584]{1,0:T(8,128)(2,1)}, u32[]{:S(2)}, u32[]{:S(2)}) collective-permute-start(bf16[256,3584]{1,0:T(8,128)(2,1)} %constant_dynamic-update-slice_fusion), channel_id=1, source_target_pairs={{0,34},{1,35},{2,32},{3,33},{4,38},{5,39},{6,36},{7,37},{8,42},{9,... | collective-permute-start | bytes 5505032 | tf_op jit(solution)/shard_map/ppermute | solution.py:23
  82.6 48.7 %collective-permute-start.16 = (bf16[256,3584]{1,0:T(8,128)(2,1)}, bf16[256,3584]{1,0:T(8,128)(2,1)}, u32[]{:S(2)}, u32[]{:S(2)}) collective-permute-start(bf16[256,3584]{1,0:T(8,128)(2,1)} %constant_dynamic-update-slice_fusion), channel_id=1, source_target_pairs={{0,32},{1,33},{2,34},{3,35},{4,36},{5,37},{6,38},{7,39},{8,40},{9,... | collective-permute-start | bytes 5505032 | tf_op jit(solution)/shard_map/ppermute | solution.py:23
  85.5 52.8 %collective-permute-start.19 = (bf16[256,3584]{1,0:T(8,128)(2,1)}, bf16[256,3584]{1,0:T(8,128)(2,1)}, u32[]{:S(2)}, u32[]{:S(2)}) collective-permute-start(bf16[256,3584]{1,0:T(8,128)(2,1)} %collective-permute-done.10), channel_id=1, source_target_pairs={{0,1},{1,0},{2,3},{3,2},{4,5},{5,4},{6,7},{7,6},{8,9},{9,8},{10,11... | collective-permute-start | bytes 5505032 | tf_op jit(solution)/shard_map/ppermute | solution.py:23
  85.6 52.7 %all-to-all-start.1 = ((bf16[8,32,3584]{2,1,0:T(8,128)(2,1)}), bf16[8,32,3584]{2,1,0:T(8,128)(2,1)}, u32[]{:S(2)}, u32[]{:S(2)}) async-start(bf16[8,32,3584]{2,1,0:T(8,128)(2,1)} %bitcast.25), calls=%async_computation.1 | async-start | bytes 3670016 | tf_op jit(solution)/shard_map/all_to_all | solution.py:74
  91.6 54.0 %collective-permute-start.18 = (bf16[256,3584]{1,0:T(8,128)(2,1)}, bf16[256,3584]{1,0:T(8,128)(2,1)}, u32[]{:S(2)}, u32[]{:S(2)}) collective-permute-start(bf16[256,3584]{1,0:T(8,128)(2,1)} %bitcast.78), channel_id=1, source_target_pairs={{0,1},{1,0},{2,3},{3,2},{4,5},{5,4},{6,7},{7,6},{8,9},{9,8},{10,11... | collective-permute-start | bytes 5505032 | tf_op jit(solution)/shard_map/ppermute | solution.py:23
  95.9 35.3 %copy-start = (bf16[3584,1024]{1,0:T(8,128)(2,1)}, bf16[3584,1024]{1,0:T(8,128)(2,1)S(1)}, u32[]{:S(2)}) copy-start(bf16[3584,1024]{1,0:T(8,128)(2,1)S(1)} %pad_maximum_fusion) | copy-start | bytes 22020100
  128.4 9.1 %collective-permute-start.17 = (bf16[256,512]{1,0:T(8,128)(2,1)S(1)}, bf16[256,512]{1,0:T(8,128)(2,1)S(1)}, u32[]{:S(2)}, u32[]{:S(2)}) collective-permute-start(bf16[256,512]{1,0:T(8,128)(2,1)S(1)} %fusion.46), channel_id=1, source_target_pairs={{0,2},{1,3},{2,0},{3,1},{4,6},{5,7},{6,4},{7,5},{8,10},{9,11},{10,... | collective-permute-start | bytes 786440 | tf_op jit(solution)/shard_map/ppermute | solution.py:23
  143.0 12.9 %collective-permute-start.20 = (bf16[256,512]{1,0:T(8,128)(2,1)}, bf16[256,512]{1,0:T(8,128)(2,1)}, u32[]{:S(2)}, u32[]{:S(2)}) collective-permute-start(bf16[256,512]{1,0:T(8,128)(2,1)} %fusion.22), channel_id=1, source_target_pairs={{0,2},{1,3},{2,0},{3,1},{4,6},{5,7},{6,4},{7,5},{8,10},{9,11},{10,... | collective-permute-start | bytes 786440 | tf_op jit(solution)/shard_map/ppermute | solution.py:23
  150.6 57.4 %all-to-all-start = ((bf16[8,32,3584]{2,1,0:T(8,128)(2,1)}), bf16[8,32,3584]{2,1,0:T(8,128)(2,1)S(1)}, u32[]{:S(2)}, u32[]{:S(2)}) async-start(bf16[8,32,3584]{2,1,0:T(8,128)(2,1)} %bitcast.64), calls=%async_computation | async-start | bytes 3670016 | tf_op jit(solution)/shard_map/all_to_all | solution.py:74
  157.2 47.2 %slice-start = ((s8[7340032]{0:T(1024)(128)(4,1)}), s8[4194304]{0:T(1024)(128)(4,1)S(1)}, s32[]{:S(2)}) async-start(s8[7340032]{0:T(1024)(128)(4,1)} %bitcast.59), calls=%async_computation.3 | async-start | bytes 8388608
  162.6 41.8 %collective-permute-start.21 = (bf16[256,3584]{1,0:T(8,128)(2,1)S(1)}, bf16[256,3584]{1,0:T(8,128)(2,1)S(1)}, u32[]{:S(2)}, u32[]{:S(2)}) collective-permute-start(bf16[256,3584]{1,0:T(8,128)(2,1)S(1)} %convolution_convert_fusion), channel_id=1, source_target_pairs={{0,2},{1,3},{2,0},{3,1},{4,6},{5,7},{6,4},{7,5},{8,10},{9,11},{10,... | collective-permute-start | bytes 5505032 | tf_op jit(solution)/shard_map/ppermute | solution.py:23
  163.9 40.6 %slice-start.1 = ((s8[7340032]{0:T(1024)(128)(4,1)}), s8[3145728]{0:T(1024)(128)(4,1)S(1)}, s32[]{:S(2)}) async-start(s8[7340032]{0:T(1024)(128)(4,1)} %bitcast.59), calls=%async_computation.4 | async-start | bytes 6291456
  167.6 36.6 %collective-permute-start.22 = (f32[256]{0:T(256)S(1)}, f32[256]{0:T(256)S(1)}, u32[]{:S(2)}, u32[]{:S(2)}) collective-permute-start(f32[256]{0:T(256)S(1)} %get-tuple-element.43), channel_id=1, source_target_pairs={{0,2},{1,3},{2,0},{3,1},{4,6},{5,7},{6,4},{7,5},{8,10},{9,11},{10,... | collective-permute-start | bytes 3080 | tf_op jit(solution)/shard_map/ppermute | solution.py:23
  208.0 8.2 %copy-start.5 = (s32[1,128,1]{1,2,0:T(1,128)S(1)}, s32[1,128,1]{1,2,0:T(1,128)}, u32[]{:S(2)}) copy-start(s32[1,128,1]{1,2,0:T(1,128)} %param.12) | copy-start | bytes 1540
  208.0 27.0 %copy-start.6 = (f32[1,128]{1,0:T(1,128)S(1)}, f32[1,128]{1,0:T(1,128)}, u32[]{:S(2)}) copy-start(f32[1,128]{1,0:T(1,128)} %param.13) | copy-start | bytes 1540
  209.2 50.7 %all-to-all-start.2 = ((bf16[8,32,3712]{2,1,0:T(8,128)(2,1)}), bf16[8,32,3712]{2,1,0:T(8,128)(2,1)S(1)}, u32[]{:S(2)}, u32[]{:S(2)}) async-start(bf16[8,32,3712]{2,1,0:T(8,128)(2,1)} %bitcast.27), calls=%async_computation.2 | async-start | bytes 3801088 | tf_op jit(solution)/shard_map/all_to_all | solution.py:74
  216.1 18.9 %collective-permute-start.15 = (bf16[128,3584]{1,0:T(8,128)(2,1)}, bf16[128,3584]{1,0:T(8,128)(2,1)}, u32[]{:S(2)}, u32[]{:S(2)}) collective-permute-start(bf16[128,3584]{1,0:T(8,128)(2,1)} %bitcast.65), channel_id=1, source_target_pairs={{0,32},{1,33},{2,34},{3,35},{4,36},{5,37},{6,38},{7,39},{8,40},{9,... | collective-permute-start | bytes 2752520 | tf_op jit(solution)/shard_map/ppermute | solution.py:23
  (6 other events, 26.2 us)

commit v2 on v1

--- a/solution.py
+++ b/solution.py
@@ -103,7 +103,7 @@
     plane = place // WS
     onward_keys = keys_of((onward_route - plane + planes) % planes, planes, capacity)
     packed = pack(forward_input[0], onward_keys, slots)
-    order = [distance for pair in zip(range(planes // 2, planes), range(planes // 2 - 1, -1, -1)) for distance in pair]
+    order = sorted(range(planes), key=lambda d: (d != planes // 2, d != 0, -min(d, planes - d)))
     arrived = {d: onward(packed[d * capacity:(d + 1) * capacity], d) for d in order}
     backward_packed, arrived[order[2]] = lax.optimization_barrier(
         (pack(upstream, backward_keys, slots), arrived[order[2]])
@@ -165,8 +165,10 @@
 
     far_terms, far_share = back_of(back_far.astype(jnp.float32), g[slots:], u[slots:])
     far_terms, backward_rows = lax.optimization_barrier((far_terms, backward_rows))
-    far_part = dot_last(far_terms, gates)
-    far_part = swap_half(far_part.astype(jnp.bfloat16))
+    middle = gates.shape[0] // 2
+    far_part = jnp.concatenate(
+        [swap_half(dot_last(far_terms, rows).astype(jnp.bfloat16)) for rows in (gates[:middle], gates[middle:])], axis=1
+    )
     far_share = swap_half(far_share)
     near_terms, near_share = back_of(dot_last(backward_rows, down[:near]), g[:slots], u[:slots])
     near_part = dot_last(near_terms, gates)

time: 263 us -> 261 us (level)
  starting transfers between devices: 76.5 us -> 64.7 us
  waiting for transfers between devices: 126 us -> 134 us
    ppermute x23 -> x24, starting transfers between devices: 59 us -> 46.7 us  [send(): return lax.ppermute(value, AXES, pairs)]
    ppermute x23 -> x24, waiting for transfers between devices: 104 us -> 112 us  [send(): return lax.ppermute(value, AXES, pairs)]
    dot_general x4 -> x5, matrix products: 15.8 us -> 16.9 us  [dot_last(): lax.dot_general(a, b, (((1,), (1,)), ((), ())), preferred_element_type=jn...]
  transfers between devices with their start and end apart: 26 -> 27, of which waited for: 12 -> 14; matrix products, arithmetic and copies ran while one was open for 21% -> 22% of each run, Pallas kernels for 0% -> 0%
where the time goes in v2:
time: 261 us; the launch traced here: 260 us
  waiting for transfers between devices  134 us (51%)
  starting transfers between devices  64.7 us (25%)
  matrix products  35 us (13%)
  other arithmetic  13.5 us (5%)
  local copies, waits for them, and re-layouts  11.6 us (4%)
    ppermute x24, waiting for transfers between devices, send(): return lax.ppermute(value, AXES, pairs)  112 us
    ppermute x24, starting transfers between devices, send(): return lax.ppermute(value, AXES, pairs)  46.7 us
    all_to_all x3, waiting for transfers between devices, exchange(): lax.all_to_all(rows, 'expert', 0, 0, axis_index_groups=groups, tiled=True)  21.8 us
    dot_general x7, matrix products, dot(): return jnp.dot(a, b, preferred_element_type=jnp.float32)  18.2 us
    all_to_all x3, starting transfers between devices, exchange(): lax.all_to_all(rows, 'expert', 0, 0, axis_index_groups=groups, tiled=True)  17.9 us
    dot_general x5, matrix products, dot_last(): lax.dot_general(a, b, (((1,), (1,)), ((), ())), preferred_element_type=jn...  16.9 us
    unnamed x31, local copies, waits for them, and re-layouts  7.11 us
  transfers between devices with their start and end apart: 27, of which 14 were waited for; matrix products, arithmetic and copies ran while one was open for 22% of the time, Pallas kernels for 0%

profile of v2, /device:TPU:2, one launch (start us, length us, event | category | flops | bytes accessed | tf_op | source)
XLA Modules:
  0.0 260.0 jit_solution(16641288989243518394)
XLA Ops:
  0.6 2.3 collective-permute-start
  3.0 2.2 collective-permute-start.4
  5.2 2.1 collective-permute-start.10
  18.0 4.3 %collective-permute-start.3 = (bf16[32,3584]{1,0:T(8,128)(2,1)}, bf16[32,3584]{1,0:T(8,128)(2,1)S(1)}, u32[]{:S(2)}, u32[]{:S(2)}) collective-permute-start(bf16[32,3584]{1,0:T(8,128)(2,1)} %get-tuple-element.50), channel_id=1, source_target_pairs={{0,8},{1,9},{2,10},{3,11},{4,12},{5,13},{6,14},{7,15},{8,16},{9,17... | collective-permute-start | bytes 688136 | tf_op jit(solution)/shard_map/ppermute | solution.py:23
  22.8 8.4 %collective-permute-start.5 = (bf16[32,3584]{1,0:T(8,128)(2,1)}, bf16[32,3584]{1,0:T(8,128)(2,1)S(1)}, u32[]{:S(2)}, u32[]{:S(2)}) collective-permute-start(bf16[32,3584]{1,0:T(8,128)(2,1)} %get-tuple-element.49), channel_id=1, source_target_pairs={{0,12},{1,13},{2,14},{3,15},{4,16},{5,17},{6,18},{7,19},{8,20},{9,... | collective-permute-start | bytes 688136 | tf_op jit(solution)/shard_map/ppermute | solution.py:23
  33.2 5.6 %collective-permute-start.6 = (bf16[32,3584]{1,0:T(8,128)(2,1)}, bf16[32,3584]{1,0:T(8,128)(2,1)S(1)}, u32[]{:S(2)}, u32[]{:S(2)}) collective-permute-start(bf16[32,3584]{1,0:T(8,128)(2,1)} %get-tuple-element.48), channel_id=1, source_target_pairs={{0,16},{1,17},{2,18},{3,19},{4,20},{5,21},{6,22},{7,23},{8,24},{9,... | collective-permute-start | bytes 688136 | tf_op jit(solution)/shard_map/ppermute | solution.py:23
  39.4 8.8 %collective-permute-done.3 = bf16[32,3584]{1,0:T(8,128)(2,1)S(1)} collective-permute-done((bf16[32,3584]{1,0:T(8,128)(2,1)}, bf16[32,3584]{1,0:T(8,128)(2,1)S(1)}, u32[]{:S(2)}, u32[]{:S(2)}) %collective-permute-start.3) | collective-permute-done | bytes 229408 | tf_op jit(solution)/shard_map/ppermute | solution.py:23
  48.2 3.6 %collective-permute-start.7 = (bf16[32,3584]{1,0:T(8,128)(2,1)}, bf16[32,3584]{1,0:T(8,128)(2,1)S(1)}, u32[]{:S(2)}, u32[]{:S(2)}) collective-permute-start(bf16[32,3584]{1,0:T(8,128)(2,1)} %get-tuple-element.47), channel_id=1, source_target_pairs={{0,20},{1,21},{2,22},{3,23},{4,24},{5,25},{6,26},{7,27},{8,28},{9,... | collective-permute-start | bytes 688136 | tf_op jit(solution)/shard_map/ppermute | solution.py:23
  56.3 2.5 collective-permute-done.6
  59.5 8.8 %collective-permute-done.7 = bf16[32,3584]{1,0:T(8,128)(2,1)S(1)} collective-permute-done((bf16[32,3584]{1,0:T(8,128)(2,1)}, bf16[32,3584]{1,0:T(8,128)(2,1)S(1)}, u32[]{:S(2)}, u32[]{:S(2)}) %collective-permute-start.7) | collective-permute-done | bytes 229408 | tf_op jit(solution)/shard_map/ppermute | solution.py:23
  69.1 7.5 %collective-permute-done.8 = bf16[32,3584]{1,0:T(8,128)(2,1)S(1)} collective-permute-done((bf16[32,3584]{1,0:T(8,128)(2,1)S(1)}, bf16[32,3584]{1,0:T(8,128)(2,1)S(1)}, u32[]{:S(2)}, u32[]{:S(2)}) %collective-permute-start.8) | collective-permute-done | bytes 229408 | tf_op jit(solution)/shard_map/ppermute | solution.py:23
  82.6 2.9 %collective-permute-start.16 = (bf16[256,3584]{1,0:T(8,128)(2,1)}, bf16[256,3584]{1,0:T(8,128)(2,1)}, u32[]{:S(2)}, u32[]{:S(2)}) collective-permute-start(bf16[256,3584]{1,0:T(8,128)(2,1)} %constant_dynamic-update-slice_fusion), channel_id=1, source_target_pairs={{0,32},{1,33},{2,34},{3,35},{4,36},{5,37},{6,38},{7,39},{8,40},{9,... | collective-permute-start | bytes 5505032 | tf_op jit(solution)/shard_map/ppermute | solution.py:23
  85.6 5.5 %all-to-all-start.1 = ((bf16[8,32,3584]{2,1,0:T(8,128)(2,1)}), bf16[8,32,3584]{2,1,0:T(8,128)(2,1)}, u32[]{:S(2)}, u32[]{:S(2)}) async-start(bf16[8,32,3584]{2,1,0:T(8,128)(2,1)} %bitcast.25), calls=%async_computation.1 | async-start | bytes 3670016 | tf_op jit(solution)/shard_map/all_to_all | solution.py:74
  92.1 4.1 %pad_maximum_fusion = bf16[3584,1024]{1,0:T(8,128)(2,1)S(1)} fusion(bf16[3584,256]{1,0:T(8,128)(2,1)} %collective-permute-done.14, bf16[3584,256]{1,0:T(8,128)(2,1)} %bitcast.6, bf16[3584,256]{1,0:T(8,128)(2,1)} %collective-permute-done.13, bf16[3584,256]{1,0:T(8,128)(2,1)} %bitcast.5), kind=kLoop, calls=%fused_computation.3 | loop fusion | flops 29360128 | bytes 14680064 | tf_op jit(solution)/shard_map/concatenate | solution.py:131
  96.2 28.5 %collective-permute-done.11 = bf16[256,3584]{1,0:T(8,128)(2,1)} collective-permute-done((bf16[256,3584]{1,0:T(8,128)(2,1)}, bf16[256,3584]{1,0:T(8,128)(2,1)}, u32[]{:S(2)}, u32[]{:S(2)}) %collective-permute-start.11) | collective-permute-done | bytes 1835040 | tf_op jit(solution)/shard_map/ppermute | solution.py:23
  124.7 3.6 %fusion.87 = f32[256,1024]{1,0:T(8,128)S(1)} fusion(bf16[256,3584]{1,0:T(8,128)(2,1)} %collective-permute-done.11, bf16[3584,1024]{1,0:T(8,128)(2,1)S(1)} %pad_maximum_fusion), kind=kOutput, calls=%fused_computation.167 | convolution fusion | flops 1879048192 | bytes 10223616 | tf_op jit(solution)/shard_map/dot_general | solution.py:47
  128.4 2.8 %collective-permute-start.17 = (bf16[256,512]{1,0:T(8,128)(2,1)S(1)}, bf16[256,512]{1,0:T(8,128)(2,1)S(1)}, u32[]{:S(2)}, u32[]{:S(2)}) collective-permute-start(bf16[256,512]{1,0:T(8,128)(2,1)S(1)} %fusion.56), channel_id=1, source_target_pairs={{0,2},{1,3},{2,0},{3,1},{4,6},{5,7},{6,4},{7,5},{8,10},{9,11},{10,... | collective-permute-start | bytes 786440 | tf_op jit(solution)/shard_map/ppermute | solution.py:23
  131.2 3.6 %fusion.88 = f32[256,1024]{1,0:T(8,128)S(1)} fusion(bf16[256,3584]{1,0:T(8,128)(2,1)} %collective-permute-done.16, bf16[3584,1024]{1,0:T(8,128)(2,1)S(1)} %pad_maximum_fusion), kind=kOutput, calls=%fused_computation.168 | convolution fusion | flops 1879048192 | bytes 10223616 | tf_op jit(solution)/shard_map/dot_general | solution.py:47
  134.9 2.6 %collective-permute-done.17 = bf16[256,512]{1,0:T(8,128)(2,1)S(1)} collective-permute-done((bf16[256,512]{1,0:T(8,128)(2,1)S(1)}, bf16[256,512]{1,0:T(8,128)(2,1)S(1)}, u32[]{:S(2)}, u32[]{:S(2)}) %collective-permute-start.17) | collective-permute-done | bytes 262176 | tf_op jit(solution)/shard_map/ppermute | solution.py:23
  138.4 4.6 %fusion.32 = bf16[256,512]{1,0:T(8,128)(2,1)} fusion(bf16[256,3584]{1,0:T(8,128)(2,1)} %bitcast.26, bf16[256,3584]{1,0:T(8,128)(2,1)} %collective-permute-done.19, bf16[256,3584]{1,0:T(8,128)(2,1)} %collective-permute-done.10), kind=kOutput, calls=%fused_computation.37 | convolution fusion | flops 946995200 | bytes 5767168 | tf_op jit(solution)/shard_map/dot_general | solution.py:51
  142.9 2.7 %collective-permute-start.20 = (bf16[256,512]{1,0:T(8,128)(2,1)}, bf16[256,512]{1,0:T(8,128)(2,1)}, u32[]{:S(2)}, u32[]{:S(2)}) collective-permute-start(bf16[256,512]{1,0:T(8,128)(2,1)} %fusion.32), channel_id=1, source_target_pairs={{0,2},{1,3},{2,0},{3,1},{4,6},{5,7},{6,4},{7,5},{8,10},{9,11},{10,... | collective-permute-start | bytes 786440 | tf_op jit(solution)/shard_map/ppermute | solution.py:23
  145.6 5.0 %fusion.8 = bf16[256,3584]{1,0:T(8,128)(2,1)} fusion(bf16[256,1024]{1,0:T(8,128)(2,1)S(1)} %bitcast_select_fusion, bf16[256,3584]{1,0:T(8,128)(2,1)} %collective-permute-done.19, bf16[256,3584]{1,0:T(8,128)(2,1)} %collective-permute-done.10, bf16[256,3584]{1,0:T(8,128)(2,1)} %collective-permute-done.18, bf16[256,3584]{1,0:T(8,128)(2,1)S(1)} %bitcast.79), kind=kOutput, calls=%fused_computation.13 | convolution fusion | flops 1909325824 | bytes 9699328 | tf_op jit(solution)/shard_map/dot_general | solution.py:47
  150.6 5.5 %all-to-all-start = ((bf16[8,32,3584]{2,1,0:T(8,128)(2,1)}), bf16[8,32,3584]{2,1,0:T(8,128)(2,1)S(1)}, u32[]{:S(2)}, u32[]{:S(2)}) async-start(bf16[8,32,3584]{2,1,0:T(8,128)(2,1)} %bitcast.64), calls=%async_computation | async-start | bytes 3670016 | tf_op jit(solution)/shard_map/all_to_all | solution.py:74
  157.5 3.2 %fusion.24 = bf16[256,1792]{1,0:T(8,128)(2,1)S(1)} fusion(bf16[256,1024]{1,0:T(8,128)(2,1)S(1)} %pad_maximum_fusion.4, bf16[3584,1024]{1,0:T(8,128)(2,1)} %copy-done), kind=kOutput, calls=%fused_computation.30 | convolution fusion | flops 939982848 | bytes 5111808 | tf_op jit(solution)/shard_map/dot_general | solution.py:51
  161.6 3.4 %fusion.27 = bf16[256,1792]{1,0:T(8,128)(2,1)S(1)} fusion(bf16[256,1024]{1,0:T(8,128)(2,1)S(1)} %pad_maximum_fusion.4, bf16[3584,1024]{1,0:T(8,128)(2,1)} %copy-done), kind=kOutput, calls=%fused_computation.31 | convolution fusion | flops 939982848 | bytes 5111808 | tf_op jit(solution)/shard_map/dot_general | solution.py:51
  165.0 3.0 %collective-permute-start.22 = (bf16[256,1792]{1,0:T(8,128)(2,1)S(1)}, bf16[256,1792]{1,0:T(8,128)(2,1)S(1)}, u32[]{:S(2)}, u32[]{:S(2)}) collective-permute-start(bf16[256,1792]{1,0:T(8,128)(2,1)S(1)} %fusion.27), channel_id=1, source_target_pairs={{0,2},{1,3},{2,0},{3,1},{4,6},{5,7},{6,4},{7,5},{8,10},{9,11},{10,... | collective-permute-start | bytes 2752520 | tf_op jit(solution)/shard_map/ppermute | solution.py:23
  168.0 3.6 %fusion.46 = (f32[256]{0:T(256)S(1)}, f32[256]{0:T(256)S(1)}, bf16[256,512]{1,0:T(8,128)(2,1)S(1)}, bf16[256,512]{1,0:T(8,128)(2,1)S(1)}) fusion(bf16[256,512]{1,0:T(8,128)(2,1)} %collective-permute-done.20, bf16[512,256]{1,0:T(8,128)(2,1)S(1)} %copy-done.2, bf16[512,256]{1,0:T(8,128)(2,1)S(1)} %get-tuple-element.58, ...), kind=kOutput, calls=%fused_computation.62 | convolution fusion | flops 952630784 | bytes 7342080 | tf_op jit(solution)/shard_map/dot_general | solution.py:51
  172.5 29.6 %collective-permute-done.23 = f32[256]{0:T(256)S(1)} collective-permute-done((f32[256]{0:T(256)S(1)}, f32[256]{0:T(256)S(1)}, u32[]{:S(2)}, u32[]{:S(2)}) %collective-permute-start.23) | collective-permute-done | bytes 1056 | tf_op jit(solution)/shard_map/ppermute | solution.py:23
  207.1 6.9 %all-to-all-start.2 = ((bf16[8,32,3712]{2,1,0:T(8,128)(2,1)}), bf16[8,32,3712]{2,1,0:T(8,128)(2,1)S(1)}, u32[]{:S(2)}, u32[]{:S(2)}) async-start(bf16[8,32,3712]{2,1,0:T(8,128)(2,1)} %bitcast.27), calls=%async_computation.2 | async-start | bytes 3801088 | tf_op jit(solution)/shard_map/all_to_all | solution.py:74
  214.5 18.4 %collective-permute-done.15 = bf16[128,3584]{1,0:T(8,128)(2,1)} collective-permute-done((bf16[128,3584]{1,0:T(8,128)(2,1)}, bf16[128,3584]{1,0:T(8,128)(2,1)}, u32[]{:S(2)}, u32[]{:S(2)}) %collective-permute-start.15) | collective-permute-done | bytes 917536 | tf_op jit(solution)/shard_map/ppermute | solution.py:23
  232.9 3.1 %fusion.35 = bf16[1,128,3584]{2,1,0:T(8,128)(2,1)} fusion(bf16[128,3584]{1,0:T(8,128)(2,1)} %collective-permute-done.15, bf16[256,3584]{1,0:T(8,128)(2,1)} %bitcast.61, f32[128]{0:T(128)S(1)} %bitcast.74, s32[128]{0:T(128)S(1)} %multiply_add_fusion), kind=kOutput, calls=%fused_computation.39 | convolution fusion | flops 236748800 | bytes 3671040 | tf_op jit(solution)/shard_map/dot_general | solution.py:47
  236.0 21.8 %all-to-all-done.2 = bf16[8,32,3712]{2,1,0:T(8,128)(2,1)S(1)} async-done(((bf16[8,32,3712]{2,1,0:T(8,128)(2,1)}), bf16[8,32,3712]{2,1,0:T(8,128)(2,1)S(1)}, u32[]{:S(2)}, u32[]{:S(2)}) %all-to-all-start.2) | async-done | bytes 1900576 | tf_op jit(solution)/shard_map/all_to_all | solution.py:74
  (112 shorter events, 38.6 us)
Async XLA Ops:
  0.6 10.4 %copy-start.3 = (bf16[1,128,3584]{2,1,0:T(8,128)(2,1)S(1)}, bf16[1,128,3584]{2,1,0:T(8,128)(2,1)}, u32[]{:S(2)}) copy-start(bf16[1,128,3584]{2,1,0:T(8,128)(2,1)} %param.11) | copy-start | bytes 2752516
  0.6 9.9 %collective-permute-start = (s32[128]{0:T(128)}, s32[128]{0:T(128)S(1)}, u32[]{:S(2)}, u32[]{:S(2)}) collective-permute-start(s32[128]{0:T(128)} %bitcast.71), channel_id=1, source_target_pairs={{0,224},{1,225},{2,226},{3,227},{4,228},{5,229},{6,230},{7,231},{8... | collective-permute-start | bytes 1544 | tf_op jit(solution)/shard_map/ppermute | solution.py:23
  3.0 49.5 %collective-permute-start.4 = (bf16[128,3584]{1,0:T(8,128)(2,1)}, bf16[128,3584]{1,0:T(8,128)(2,1)S(1)}, u32[]{:S(2)}, u32[]{:S(2)}) collective-permute-start(bf16[128,3584]{1,0:T(8,128)(2,1)} %bitcast.81), channel_id=1, source_target_pairs={{0,224},{1,225},{2,226},{3,227},{4,228},{5,229},{6,230},{7,231},{8... | collective-permute-start | bytes 2752520 | tf_op jit(solution)/shard_map/ppermute | solution.py:23
  5.2 74.7 %collective-permute-start.10 = (bf16[256,3584]{1,0:T(8,128)(2,1)}, bf16[256,3584]{1,0:T(8,128)(2,1)}, u32[]{:S(2)}, u32[]{:S(2)}) collective-permute-start(bf16[256,3584]{1,0:T(8,128)(2,1)} %bitcast.77), channel_id=1, source_target_pairs={{0,2},{1,3},{2,0},{3,1},{4,6},{5,7},{6,4},{7,5},{8,10},{9,11},{10,... | collective-permute-start | bytes 5505032 | tf_op jit(solution)/shard_map/ppermute | solution.py:23
  12.8 10.0 %collective-permute-start.1 = (bf16[32,3584]{1,0:T(8,128)(2,1)}, bf16[32,3584]{1,0:T(8,128)(2,1)}, u32[]{:S(2)}, u32[]{:S(2)}) collective-permute-start(bf16[32,3584]{1,0:T(8,128)(2,1)} %get-tuple-element.52), channel_id=1, source_target_pairs={{0,0},{1,1},{2,2},{3,3},{4,4},{5,5},{6,6},{7,7},{8,8},{9,9},{10,10... | collective-permute-start | bytes 688136 | tf_op jit(solution)/shard_map/ppermute | solution.py:23
  16.0 17.1 %collective-permute-start.2 = (bf16[32,3584]{1,0:T(8,128)(2,1)}, bf16[32,3584]{1,0:T(8,128)(2,1)S(1)}, u32[]{:S(2)}, u32[]{:S(2)}) collective-permute-start(bf16[32,3584]{1,0:T(8,128)(2,1)} %get-tuple-element.51), channel_id=1, source_target_pairs={{0,4},{1,5},{2,6},{3,7},{4,8},{5,9},{6,10},{7,11},{8,12},{9,13},{1... | collective-permute-start | bytes 688136 | tf_op jit(solution)/shard_map/ppermute | solution.py:23
  18.0 30.2 %collective-permute-start.3 = (bf16[32,3584]{1,0:T(8,128)(2,1)}, bf16[32,3584]{1,0:T(8,128)(2,1)S(1)}, u32[]{:S(2)}, u32[]{:S(2)}) collective-permute-start(bf16[32,3584]{1,0:T(8,128)(2,1)} %get-tuple-element.50), channel_id=1, source_target_pairs={{0,8},{1,9},{2,10},{3,11},{4,12},{5,13},{6,14},{7,15},{8,16},{9,17... | collective-permute-start | bytes 688136 | tf_op jit(solution)/shard_map/ppermute | solution.py:23
  22.8 32.8 %collective-permute-start.5 = (bf16[32,3584]{1,0:T(8,128)(2,1)}, bf16[32,3584]{1,0:T(8,128)(2,1)S(1)}, u32[]{:S(2)}, u32[]{:S(2)}) collective-permute-start(bf16[32,3584]{1,0:T(8,128)(2,1)} %get-tuple-element.49), channel_id=1, source_target_pairs={{0,12},{1,13},{2,14},{3,15},{4,16},{5,17},{6,18},{7,19},{8,20},{9,... | collective-permute-start | bytes 688136 | tf_op jit(solution)/shard_map/ppermute | solution.py:23
  33.2 25.7 %collective-permute-start.6 = (bf16[32,3584]{1,0:T(8,128)(2,1)}, bf16[32,3584]{1,0:T(8,128)(2,1)S(1)}, u32[]{:S(2)}, u32[]{:S(2)}) collective-permute-start(bf16[32,3584]{1,0:T(8,128)(2,1)} %get-tuple-element.48), channel_id=1, source_target_pairs={{0,16},{1,17},{2,18},{3,19},{4,20},{5,21},{6,22},{7,23},{8,24},{9,... | collective-permute-start | bytes 688136 | tf_op jit(solution)/shard_map/ppermute | solution.py:23
  48.2 20.1 %collective-permute-start.7 = (bf16[32,3584]{1,0:T(8,128)(2,1)}, bf16[32,3584]{1,0:T(8,128)(2,1)S(1)}, u32[]{:S(2)}, u32[]{:S(2)}) collective-permute-start(bf16[32,3584]{1,0:T(8,128)(2,1)} %get-tuple-element.47), channel_id=1, source_target_pairs={{0,20},{1,21},{2,22},{3,23},{4,24},{5,25},{6,26},{7,27},{8,28},{9,... | collective-permute-start | bytes 688136 | tf_op jit(solution)/shard_map/ppermute | solution.py:23
  52.5 24.1 %collective-permute-start.8 = (bf16[32,3584]{1,0:T(8,128)(2,1)S(1)}, bf16[32,3584]{1,0:T(8,128)(2,1)S(1)}, u32[]{:S(2)}, u32[]{:S(2)}) collective-permute-start(bf16[32,3584]{1,0:T(8,128)(2,1)S(1)} %get-tuple-element.46), channel_id=1, source_target_pairs={{0,24},{1,25},{2,26},{3,27},{4,28},{5,29},{6,30},{7,31},{8,0},{9,1... | collective-permute-start | bytes 688136 | tf_op jit(solution)/shard_map/ppermute | solution.py:23
  55.6 23.6 %collective-permute-start.9 = (bf16[32,3584]{1,0:T(8,128)(2,1)S(1)}, bf16[32,3584]{1,0:T(8,128)(2,1)S(1)}, u32[]{:S(2)}, u32[]{:S(2)}) collective-permute-start(bf16[32,3584]{1,0:T(8,128)(2,1)S(1)} %get-tuple-element.45), channel_id=1, source_target_pairs={{0,28},{1,29},{2,30},{3,31},{4,0},{5,1},{6,2},{7,3},{8,4},{9,5},{1... | collective-permute-start | bytes 688136 | tf_op jit(solution)/shard_map/ppermute | solution.py:23
  79.9 1.9 collective-permute-start.12
  81.8 10.0 %collective-permute-start.13 = (bf16[3584,256]{1,0:T(8,128)(2,1)}, bf16[3584,256]{1,0:T(8,128)(2,1)}, u32[]{:S(2)}, u32[]{:S(2)}) collective-permute-start(bf16[3584,256]{1,0:T(8,128)(2,1)} %bitcast.5), channel_id=1, source_target_pairs={{0,1},{1,0},{2,3},{3,2},{4,5},{5,4},{6,7},{7,6},{8,9},{9,8},{10,11... | collective-permute-start | bytes 5505032 | tf_op jit(solution)/shard_map/ppermute | solution.py:23
  82.0 10.1 %collective-permute-start.14 = (bf16[3584,256]{1,0:T(8,128)(2,1)}, bf16[3584,256]{1,0:T(8,128)(2,1)}, u32[]{:S(2)}, u32[]{:S(2)}) collective-permute-start(bf16[3584,256]{1,0:T(8,128)(2,1)} %bitcast.6), channel_id=1, source_target_pairs={{0,1},{1,0},{2,3},{3,2},{4,5},{5,4},{6,7},{7,6},{8,9},{9,8},{10,11... | collective-permute-start | bytes 5505032 | tf_op jit(solution)/shard_map/ppermute | solution.py:23
  82.3 42.4 %collective-permute-start.11 = (bf16[256,3584]{1,0:T(8,128)(2,1)}, bf16[256,3584]{1,0:T(8,128)(2,1)}, u32[]{:S(2)}, u32[]{:S(2)}) collective-permute-start(bf16[256,3584]{1,0:T(8,128)(2,1)} %constant_dynamic-update-slice_fusion), channel_id=1, source_target_pairs={{0,34},{1,35},{2,32},{3,33},{4,38},{5,39},{6,36},{7,37},{8,42},{9,... | collective-permute-start | bytes 5505032 | tf_op jit(solution)/shard_map/ppermute | solution.py:23
  82.6 48.6 %collective-permute-start.16 = (bf16[256,3584]{1,0:T(8,128)(2,1)}, bf16[256,3584]{1,0:T(8,128)(2,1)}, u32[]{:S(2)}, u32[]{:S(2)}) collective-permute-start(bf16[256,3584]{1,0:T(8,128)(2,1)} %constant_dynamic-update-slice_fusion), channel_id=1, source_target_pairs={{0,32},{1,33},{2,34},{3,35},{4,36},{5,37},{6,38},{7,39},{8,40},{9,... | collective-permute-start | bytes 5505032 | tf_op jit(solution)/shard_map/ppermute | solution.py:23
  85.5 52.8 %collective-permute-start.19 = (bf16[256,3584]{1,0:T(8,128)(2,1)}, bf16[256,3584]{1,0:T(8,128)(2,1)}, u32[]{:S(2)}, u32[]{:S(2)}) collective-permute-start(bf16[256,3584]{1,0:T(8,128)(2,1)} %collective-permute-done.10), channel_id=1, source_target_pairs={{0,1},{1,0},{2,3},{3,2},{4,5},{5,4},{6,7},{7,6},{8,9},{9,8},{10,11... | collective-permute-start | bytes 5505032 | tf_op jit(solution)/shard_map/ppermute | solution.py:23
  85.6 52.7 %all-to-all-start.1 = ((bf16[8,32,3584]{2,1,0:T(8,128)(2,1)}), bf16[8,32,3584]{2,1,0:T(8,128)(2,1)}, u32[]{:S(2)}, u32[]{:S(2)}) async-start(bf16[8,32,3584]{2,1,0:T(8,128)(2,1)} %bitcast.25), calls=%async_computation.1 | async-start | bytes 3670016 | tf_op jit(solution)/shard_map/all_to_all | solution.py:74
  91.9 53.8 %collective-permute-start.18 = (bf16[256,3584]{1,0:T(8,128)(2,1)}, bf16[256,3584]{1,0:T(8,128)(2,1)}, u32[]{:S(2)}, u32[]{:S(2)}) collective-permute-start(bf16[256,3584]{1,0:T(8,128)(2,1)} %bitcast.78), channel_id=1, source_target_pairs={{0,1},{1,0},{2,3},{3,2},{4,5},{5,4},{6,7},{7,6},{8,9},{9,8},{10,11... | collective-permute-start | bytes 5505032 | tf_op jit(solution)/shard_map/ppermute | solution.py:23
  96.2 35.0 %copy-start = (bf16[3584,1024]{1,0:T(8,128)(2,1)}, bf16[3584,1024]{1,0:T(8,128)(2,1)S(1)}, u32[]{:S(2)}) copy-start(bf16[3584,1024]{1,0:T(8,128)(2,1)S(1)} %pad_maximum_fusion) | copy-start | bytes 22020100
  128.4 9.1 %collective-permute-start.17 = (bf16[256,512]{1,0:T(8,128)(2,1)S(1)}, bf16[256,512]{1,0:T(8,128)(2,1)S(1)}, u32[]{:S(2)}, u32[]{:S(2)}) collective-permute-start(bf16[256,512]{1,0:T(8,128)(2,1)S(1)} %fusion.56), channel_id=1, source_target_pairs={{0,2},{1,3},{2,0},{3,1},{4,6},{5,7},{6,4},{7,5},{8,10},{9,11},{10,... | collective-permute-start | bytes 786440 | tf_op jit(solution)/shard_map/ppermute | solution.py:23
  142.9 13.2 %collective-permute-start.20 = (bf16[256,512]{1,0:T(8,128)(2,1)}, bf16[256,512]{1,0:T(8,128)(2,1)}, u32[]{:S(2)}, u32[]{:S(2)}) collective-permute-start(bf16[256,512]{1,0:T(8,128)(2,1)} %fusion.32), channel_id=1, source_target_pairs={{0,2},{1,3},{2,0},{3,1},{4,6},{5,7},{6,4},{7,5},{8,10},{9,11},{10,... | collective-permute-start | bytes 786440 | tf_op jit(solution)/shard_map/ppermute | solution.py:23
  150.6 55.2 %all-to-all-start = ((bf16[8,32,3584]{2,1,0:T(8,128)(2,1)}), bf16[8,32,3584]{2,1,0:T(8,128)(2,1)S(1)}, u32[]{:S(2)}, u32[]{:S(2)}) async-start(bf16[8,32,3584]{2,1,0:T(8,128)(2,1)} %bitcast.64), calls=%async_computation | async-start | bytes 3670016 | tf_op jit(solution)/shard_map/all_to_all | solution.py:74
  160.7 41.6 %collective-permute-start.21 = (bf16[256,1792]{1,0:T(8,128)(2,1)S(1)}, bf16[256,1792]{1,0:T(8,128)(2,1)S(1)}, u32[]{:S(2)}, u32[]{:S(2)}) collective-permute-start(bf16[256,1792]{1,0:T(8,128)(2,1)S(1)} %fusion.24), channel_id=1, source_target_pairs={{0,2},{1,3},{2,0},{3,1},{4,6},{5,7},{6,4},{7,5},{8,10},{9,11},{10,... | collective-permute-start | bytes 2752520 | tf_op jit(solution)/shard_map/ppermute | solution.py:23
  161.6 40.7 %slice-start = ((s8[7340032]{0:T(1024)(128)(4,1)}), s8[4194304]{0:T(1024)(128)(4,1)S(1)}, s32[]{:S(2)}) async-start(s8[7340032]{0:T(1024)(128)(4,1)} %bitcast.59), calls=%async_computation.3 | async-start | bytes 8388608
  165.0 37.3 %slice-start.1 = ((s8[7340032]{0:T(1024)(128)(4,1)}), s8[3145728]{0:T(1024)(128)(4,1)S(1)}, s32[]{:S(2)}) async-start(s8[7340032]{0:T(1024)(128)(4,1)} %bitcast.59), calls=%async_computation.4 | async-start | bytes 6291456
  165.0 37.3 %collective-permute-start.22 = (bf16[256,1792]{1,0:T(8,128)(2,1)S(1)}, bf16[256,1792]{1,0:T(8,128)(2,1)S(1)}, u32[]{:S(2)}, u32[]{:S(2)}) collective-permute-start(bf16[256,1792]{1,0:T(8,128)(2,1)S(1)} %fusion.27), channel_id=1, source_target_pairs={{0,2},{1,3},{2,0},{3,1},{4,6},{5,7},{6,4},{7,5},{8,10},{9,11},{10,... | collective-permute-start | bytes 2752520 | tf_op jit(solution)/shard_map/ppermute | solution.py:23
  171.6 30.5 %collective-permute-start.23 = (f32[256]{0:T(256)S(1)}, f32[256]{0:T(256)S(1)}, u32[]{:S(2)}, u32[]{:S(2)}) collective-permute-start(f32[256]{0:T(256)S(1)} %get-tuple-element.43), channel_id=1, source_target_pairs={{0,2},{1,3},{2,0},{3,1},{4,6},{5,7},{6,4},{7,5},{8,10},{9,11},{10,... | collective-permute-start | bytes 3080 | tf_op jit(solution)/shard_map/ppermute | solution.py:23
  205.9 27.0 %copy-start.6 = (f32[1,128]{1,0:T(1,128)S(1)}, f32[1,128]{1,0:T(1,128)}, u32[]{:S(2)}) copy-start(f32[1,128]{1,0:T(1,128)} %param.13) | copy-start | bytes 1540
  207.1 50.7 %all-to-all-start.2 = ((bf16[8,32,3712]{2,1,0:T(8,128)(2,1)}), bf16[8,32,3712]{2,1,0:T(8,128)(2,1)S(1)}, u32[]{:S(2)}, u32[]{:S(2)}) async-start(bf16[8,32,3712]{2,1,0:T(8,128)(2,1)} %bitcast.27), calls=%async_computation.2 | async-start | bytes 3801088 | tf_op jit(solution)/shard_map/all_to_all | solution.py:74
  214.0 18.9 %collective-permute-start.15 = (bf16[128,3584]{1,0:T(8,128)(2,1)}, bf16[128,3584]{1,0:T(8,128)(2,1)}, u32[]{:S(2)}, u32[]{:S(2)}) collective-permute-start(bf16[128,3584]{1,0:T(8,128)(2,1)} %bitcast.65), channel_id=1, source_target_pairs={{0,32},{1,33},{2,34},{3,35},{4,36},{5,37},{6,38},{7,39},{8,40},{9,... | collective-permute-start | bytes 2752520 | tf_op jit(solution)/shard_map/ppermute | solution.py:23
  (7 other events, 35.6 us)

commit v3 on v2

--- a/solution.py
+++ b/solution.py
@@ -165,7 +165,7 @@
 
     far_terms, far_share = back_of(back_far.astype(jnp.float32), g[slots:], u[slots:])
     far_terms, backward_rows = lax.optimization_barrier((far_terms, backward_rows))
-    middle = gates.shape[0] // 2
+    middle = gates.shape[0] * 2 // 7 // 128 * 128
     far_part = jnp.concatenate(
         [swap_half(dot_last(far_terms, rows).astype(jnp.bfloat16)) for rows in (gates[:middle], gates[middle:])], axis=1
     )

time: 261 us -> 293 us (1.12)
  waiting for transfers between devices: 134 us -> 164 us
  matrix products: 35 us -> 45 us
  starting transfers between devices: 64.7 us -> 60.4 us
  other arithmetic: 13.5 us -> 9.39 us
    ppermute x24, waiting for transfers between devices: 112 us -> 142 us  [send(): return lax.ppermute(value, AXES, pairs)]
    dot_general x7, matrix products: 18.2 us -> 26.4 us  [dot(): return jnp.dot(a, b, preferred_element_type=jnp.float32)]
    concatenate x1 -> x0, other arithmetic: 4.09 us -> none  [per_device(): jnp.concatenate([gate_first, swap_core(gate_own), up_first, swap_core(up_...]
    all_to_all x3, starting transfers between devices: 17.9 us -> 14.7 us  [exchange(): lax.all_to_all(rows, 'expert', 0, 0, axis_index_groups=groups, tiled=True)]
    unnamed x31 -> x27, local copies, waits for them, and re-layouts: 7.11 us -> 7.16 us
  transfers between devices with their start and end apart: 27 -> 27, of which waited for: 14 -> 11; matrix products, arithmetic and copies ran while one was open for 22% -> 21% of each run, Pallas kernels for 0% -> 0%
where the time goes in v3:
time: 293 us; the launch traced here: 291 us
  waiting for transfers between devices  164 us (56%)
  starting transfers between devices  60.4 us (21%)
  matrix products  45 us (15%)
  local copies, waits for them, and re-layouts  11.6 us (4%)
  other arithmetic  9.39 us (3%)
    ppermute x24, waiting for transfers between devices, send(): return lax.ppermute(value, AXES, pairs)  142 us
    ppermute x24, starting transfers between devices, send(): return lax.ppermute(value, AXES, pairs)  45.6 us
    dot_general x7, matrix products, dot(): return jnp.dot(a, b, preferred_element_type=jnp.float32)  26.4 us
    all_to_all x3, waiting for transfers between devices, exchange(): lax.all_to_all(rows, 'expert', 0, 0, axis_index_groups=groups, tiled=True)  21.8 us
    dot_general x5, matrix products, dot_last(): lax.dot_general(a, b, (((1,), (1,)), ((), ())), preferred_element_type=jn...  18.6 us
    all_to_all x3, starting transfers between devices, exchange(): lax.all_to_all(rows, 'expert', 0, 0, axis_index_groups=groups, tiled=True)  14.7 us
    unnamed x27, local copies, waits for them, and re-layouts  7.16 us
  transfers between devices with their start and end apart: 27, of which 11 were waited for; matrix products, arithmetic and copies ran while one was open for 21% of the time, Pallas kernels for 0%

profile of v3, /device:TPU:2, one launch (start us, length us, event | category | flops | bytes accessed | tf_op | source)
XLA Modules:
  0.0 291.4 jit_solution(18170863883559835155)
XLA Ops:
  0.6 2.3 collective-permute-start
  3.0 2.2 collective-permute-start.4
  5.2 2.1 collective-permute-start.10
  16.1 5.9 %collective-permute-start.9 = (bf16[32,3584]{1,0:T(8,128)(2,1)S(1)}, bf16[32,3584]{1,0:T(8,128)(2,1)S(1)}, u32[]{:S(2)}, u32[]{:S(2)}) collective-permute-start(bf16[32,3584]{1,0:T(8,128)(2,1)S(1)} %get-tuple-element.45), channel_id=1, source_target_pairs={{0,28},{1,29},{2,30},{3,31},{4,0},{5,1},{6,2},{7,3},{8,4},{9,5},{1... | collective-permute-start | bytes 688136 | tf_op jit(solution)/shard_map/ppermute | solution.py:23
  22.0 2.5 collective-permute-start.8
  24.5 3.8 %collective-permute-done.1 = bf16[32,3584]{1,0:T(8,128)(2,1)} collective-permute-done((bf16[32,3584]{1,0:T(8,128)(2,1)}, bf16[32,3584]{1,0:T(8,128)(2,1)}, u32[]{:S(2)}, u32[]{:S(2)}) %collective-permute-start.1) | collective-permute-done | bytes 229408 | tf_op jit(solution)/shard_map/ppermute | solution.py:23
  28.2 4.7 %collective-permute-start.2 = (bf16[32,3584]{1,0:T(8,128)(2,1)}, bf16[32,3584]{1,0:T(8,128)(2,1)S(1)}, u32[]{:S(2)}, u32[]{:S(2)}) collective-permute-start(bf16[32,3584]{1,0:T(8,128)(2,1)} %get-tuple-element.51), channel_id=1, source_target_pairs={{0,4},{1,5},{2,6},{3,7},{4,8},{5,9},{6,10},{7,11},{8,12},{9,13},{1... | collective-permute-start | bytes 688136 | tf_op jit(solution)/shard_map/ppermute | solution.py:23
  34.5 14.1 %collective-permute-done.2 = bf16[32,3584]{1,0:T(8,128)(2,1)S(1)} collective-permute-done((bf16[32,3584]{1,0:T(8,128)(2,1)}, bf16[32,3584]{1,0:T(8,128)(2,1)S(1)}, u32[]{:S(2)}, u32[]{:S(2)}) %collective-permute-start.2) | collective-permute-done | bytes 229408 | tf_op jit(solution)/shard_map/ppermute | solution.py:23
  49.4 10.1 %collective-permute-done.3 = bf16[32,3584]{1,0:T(8,128)(2,1)S(1)} collective-permute-done((bf16[32,3584]{1,0:T(8,128)(2,1)}, bf16[32,3584]{1,0:T(8,128)(2,1)S(1)}, u32[]{:S(2)}, u32[]{:S(2)}) %collective-permute-start.3) | collective-permute-done | bytes 229408 | tf_op jit(solution)/shard_map/ppermute | solution.py:23
  59.5 11.6 %collective-permute-start.7 = (bf16[32,3584]{1,0:T(8,128)(2,1)}, bf16[32,3584]{1,0:T(8,128)(2,1)S(1)}, u32[]{:S(2)}, u32[]{:S(2)}) collective-permute-start(bf16[32,3584]{1,0:T(8,128)(2,1)} %get-tuple-element.47), channel_id=1, source_target_pairs={{0,20},{1,21},{2,22},{3,23},{4,24},{5,25},{6,26},{7,27},{8,28},{9,... | collective-permute-start | bytes 688136 | tf_op jit(solution)/shard_map/ppermute | solution.py:23
  73.7 15.2 %collective-permute-done.5 = bf16[32,3584]{1,0:T(8,128)(2,1)S(1)} collective-permute-done((bf16[32,3584]{1,0:T(8,128)(2,1)}, bf16[32,3584]{1,0:T(8,128)(2,1)S(1)}, u32[]{:S(2)}, u32[]{:S(2)}) %collective-permute-start.5) | collective-permute-done | bytes 229408 | tf_op jit(solution)/shard_map/ppermute | solution.py:23
  89.8 11.2 %collective-permute-done.6 = bf16[32,3584]{1,0:T(8,128)(2,1)S(1)} collective-permute-done((bf16[32,3584]{1,0:T(8,128)(2,1)S(1)}, bf16[32,3584]{1,0:T(8,128)(2,1)S(1)}, u32[]{:S(2)}, u32[]{:S(2)}) %collective-permute-start.6) | collective-permute-done | bytes 229408 | tf_op jit(solution)/shard_map/ppermute | solution.py:23
  107.5 4.3 %all-to-all-start.1 = ((bf16[8,32,3584]{2,1,0:T(8,128)(2,1)}), bf16[8,32,3584]{2,1,0:T(8,128)(2,1)}, u32[]{:S(2)}, u32[]{:S(2)}) async-start(bf16[8,32,3584]{2,1,0:T(8,128)(2,1)} %bitcast.25), calls=%async_computation.1 | async-start | bytes 3670016 | tf_op jit(solution)/shard_map/all_to_all | solution.py:74
  112.7 33.9 %collective-permute-done.11 = bf16[256,3584]{1,0:T(8,128)(2,1)} collective-permute-done((bf16[256,3584]{1,0:T(8,128)(2,1)}, bf16[256,3584]{1,0:T(8,128)(2,1)}, u32[]{:S(2)}, u32[]{:S(2)}) %collective-permute-start.11) | collective-permute-done | bytes 1835040 | tf_op jit(solution)/shard_map/ppermute | solution.py:23
  146.6 7.7 %fusion.99 = f32[256,1024]{1,0:T(8,128)S(1)} fusion(bf16[256,3584]{1,0:T(8,128)(2,1)} %collective-permute-done.11, bf16[3584,256]{1,0:T(8,128)(2,1)} %collective-permute-done.14, bf16[3584,256]{1,0:T(8,128)(2,1)} %bitcast.6, bf16[3584,256]{1,0:T(8,128)(2,1)} %collective-permute-done.13, bf16[3584,256]{1,0:T(8,128)(2,1)} %bitcast.5), kind=kOutput, calls=%fused_computation.179 | convolution fusion | flops 1908408320 | bytes 10223616 | tf_op jit(solution)/shard_map/dot_general | solution.py:47
  154.5 2.8 collective-permute-start.17
  157.3 7.7 %fusion.98 = f32[256,1024]{1,0:T(8,128)S(1)} fusion(bf16[256,3584]{1,0:T(8,128)(2,1)} %collective-permute-done.16, bf16[3584,256]{1,0:T(8,128)(2,1)} %collective-permute-done.14, bf16[3584,256]{1,0:T(8,128)(2,1)} %bitcast.6, bf16[3584,256]{1,0:T(8,128)(2,1)} %collective-permute-done.13, bf16[3584,256]{1,0:T(8,128)(2,1)} %bitcast.5), kind=kOutput, calls=%fused_computation.178 | convolution fusion | flops 1908408320 | bytes 10223616 | tf_op jit(solution)/shard_map/dot_general | solution.py:47
  166.0 4.6 %fusion.44 = bf16[256,512]{1,0:T(8,128)(2,1)} fusion(bf16[256,3584]{1,0:T(8,128)(2,1)} %bitcast.26, bf16[256,3584]{1,0:T(8,128)(2,1)} %collective-permute-done.19, bf16[256,3584]{1,0:T(8,128)(2,1)} %collective-permute-done.10), kind=kOutput, calls=%fused_computation.49 | convolution fusion | flops 946995200 | bytes 5767168 | tf_op jit(solution)/shard_map/dot_general | solution.py:51
  170.6 2.3 collective-permute-start.20
  172.9 5.0 %fusion.16 = bf16[256,3584]{1,0:T(8,128)(2,1)} fusion(bf16[256,1024]{1,0:T(8,128)(2,1)S(1)} %bitcast_select_fusion, bf16[256,3584]{1,0:T(8,128)(2,1)} %collective-permute-done.19, bf16[256,3584]{1,0:T(8,128)(2,1)} %collective-permute-done.10, bf16[256,3584]{1,0:T(8,128)(2,1)} %collective-permute-done.18, bf16[256,3584]{1,0:T(8,128)(2,1)S(1)} %bitcast.74), kind=kOutput, calls=%fused_computation.21 | convolution fusion | flops 1909325824 | bytes 9699328 | tf_op jit(solution)/shard_map/dot_general | solution.py:47
  177.9 3.6 %all-to-all-start = ((bf16[8,32,3584]{2,1,0:T(8,128)(2,1)}), bf16[8,32,3584]{2,1,0:T(8,128)(2,1)S(1)}, u32[]{:S(2)}, u32[]{:S(2)}) async-start(bf16[8,32,3584]{2,1,0:T(8,128)(2,1)} %bitcast.59), calls=%async_computation | async-start | bytes 3670016 | tf_op jit(solution)/shard_map/all_to_all | solution.py:74
  182.8 3.6 %fusion.20 = bf16[256,2560]{1,0:T(8,128)(2,1)S(1)} fusion(bf16[256,1024]{1,0:T(8,128)(2,1)S(1)} %pad_maximum_fusion.4, bf16[3584,256]{1,0:T(8,128)(2,1)} %collective-permute-done.14, bf16[3584,256]{1,0:T(8,128)(2,1)} %bitcast.6, bf16[3584,256]{1,0:T(8,128)(2,1)} %collective-permute-done.13, bf16[3584,256]{1,0:T(8,128)(2,1)} %bitcast.5), kind=kOutput, calls=%fused_computation.26 | convolution fusion | flops 1363804160 | bytes 9175040 | tf_op jit(solution)/shard_map/dot_general | solution.py:51
  188.0 3.6 %fusion.58 = (f32[256]{0:T(256)S(1)}, f32[256]{0:T(256)S(1)}, bf16[256,512]{1,0:T(8,128)(2,1)S(1)}, bf16[256,512]{1,0:T(8,128)(2,1)S(1)}) fusion(bf16[256,512]{1,0:T(8,128)(2,1)} %collective-permute-done.20, bf16[512,256]{1,0:T(8,128)(2,1)S(1)} %copy-done.1, bf16[512,256]{1,0:T(8,128)(2,1)S(1)} %get-tuple-element.58, ...), kind=kOutput, calls=%fused_computation.74 | convolution fusion | flops 952630784 | bytes 7342080 | tf_op jit(solution)/shard_map/dot_general | solution.py:51
  191.6 2.4 collective-permute-start.23
  194.0 2.3 fusion.41
  197.6 22.5 %collective-permute-done.23 = f32[256]{0:T(256)S(1)} collective-permute-done((f32[256]{0:T(256)S(1)}, f32[256]{0:T(256)S(1)}, u32[]{:S(2)}, u32[]{:S(2)}) %collective-permute-start.23) | collective-permute-done | bytes 1056 | tf_op jit(solution)/shard_map/ppermute | solution.py:23
  220.3 9.4 %collective-permute-done.21 = bf16[256,1024]{1,0:T(8,128)(2,1)S(1)} collective-permute-done((bf16[256,1024]{1,0:T(8,128)(2,1)S(1)}, bf16[256,1024]{1,0:T(8,128)(2,1)S(1)}, u32[]{:S(2)}, u32[]{:S(2)}) %collective-permute-start.21) | collective-permute-done | bytes 524320 | tf_op jit(solution)/shard_map/ppermute | solution.py:23
  229.7 4.5 %fusion.19 = bf16[256,3584]{1,0:T(8,128)(2,1)S(1)} fusion(bf16[256,2560]{1,0:T(8,128)(2,1)S(1)} %collective-permute-done.22, bf16[256,1024]{1,0:T(8,128)(2,1)S(1)} %collective-permute-done.21, bf16[256,512]{1,0:T(8,128)(2,1)S(1)} %get-tuple-element.54, bf16[256,512]{1,0:T(8,128)(2,1)S(1)} %get-tuple-element.53, ...), kind=kOutput, calls=%fused_computation.24 | convolution fusion | flops 1914961920 | bytes 11534336 | tf_op jit(solution)/shard_map/dot_general | solution.py:51
  236.8 6.8 %all-to-all-start.2 = ((bf16[8,32,3712]{2,1,0:T(8,128)(2,1)}), bf16[8,32,3712]{2,1,0:T(8,128)(2,1)S(1)}, u32[]{:S(2)}, u32[]{:S(2)}) async-start(bf16[8,32,3712]{2,1,0:T(8,128)(2,1)} %bitcast.27), calls=%async_computation.2 | async-start | bytes 3801088 | tf_op jit(solution)/shard_map/all_to_all | solution.py:74
  244.1 20.0 %collective-permute-done.15 = bf16[128,3584]{1,0:T(8,128)(2,1)} collective-permute-done((bf16[128,3584]{1,0:T(8,128)(2,1)}, bf16[128,3584]{1,0:T(8,128)(2,1)}, u32[]{:S(2)}, u32[]{:S(2)}) %collective-permute-start.15) | collective-permute-done | bytes 917536 | tf_op jit(solution)/shard_map/ppermute | solution.py:23
  264.2 3.1 %fusion.47 = bf16[1,128,3584]{2,1,0:T(8,128)(2,1)} fusion(bf16[128,3584]{1,0:T(8,128)(2,1)} %collective-permute-done.15, bf16[256,3584]{1,0:T(8,128)(2,1)} %bitcast.56, f32[128]{0:T(128)S(1)} %bitcast.69, s32[128]{0:T(128)S(1)} %multiply_add_fusion), kind=kOutput, calls=%fused_computation.51 | convolution fusion | flops 236748800 | bytes 3671040 | tf_op jit(solution)/shard_map/dot_general | solution.py:47
  267.3 21.8 %all-to-all-done.2 = bf16[8,32,3712]{2,1,0:T(8,128)(2,1)S(1)} async-done(((bf16[8,32,3712]{2,1,0:T(8,128)(2,1)}), bf16[8,32,3712]{2,1,0:T(8,128)(2,1)S(1)}, u32[]{:S(2)}, u32[]{:S(2)}) %all-to-all-start.2) | async-done | bytes 1900576 | tf_op jit(solution)/shard_map/all_to_all | solution.py:74
  (106 shorter events, 32.6 us)
Async XLA Ops:
  0.6 10.4 %copy-start.2 = (bf16[1,128,3584]{2,1,0:T(8,128)(2,1)S(1)}, bf16[1,128,3584]{2,1,0:T(8,128)(2,1)}, u32[]{:S(2)}) copy-start(bf16[1,128,3584]{2,1,0:T(8,128)(2,1)} %param.11) | copy-start | bytes 2752516
  0.6 9.9 %collective-permute-start = (s32[128]{0:T(128)}, s32[128]{0:T(128)S(1)}, u32[]{:S(2)}, u32[]{:S(2)}) collective-permute-start(s32[128]{0:T(128)} %bitcast.66), channel_id=1, source_target_pairs={{0,224},{1,225},{2,226},{3,227},{4,228},{5,229},{6,230},{7,231},{8... | collective-permute-start | bytes 1544 | tf_op jit(solution)/shard_map/ppermute | solution.py:23
  3.0 68.8 %collective-permute-start.4 = (bf16[128,3584]{1,0:T(8,128)(2,1)}, bf16[128,3584]{1,0:T(8,128)(2,1)S(1)}, u32[]{:S(2)}, u32[]{:S(2)}) collective-permute-start(bf16[128,3584]{1,0:T(8,128)(2,1)} %bitcast.76), channel_id=1, source_target_pairs={{0,224},{1,225},{2,226},{3,227},{4,228},{5,229},{6,230},{7,231},{8... | collective-permute-start | bytes 2752520 | tf_op jit(solution)/shard_map/ppermute | solution.py:23
  5.2 98.6 %collective-permute-start.10 = (bf16[256,3584]{1,0:T(8,128)(2,1)}, bf16[256,3584]{1,0:T(8,128)(2,1)}, u32[]{:S(2)}, u32[]{:S(2)}) collective-permute-start(bf16[256,3584]{1,0:T(8,128)(2,1)} %bitcast.72), channel_id=1, source_target_pairs={{0,2},{1,3},{2,0},{3,1},{4,6},{5,7},{6,4},{7,5},{8,10},{9,11},{10,... | collective-permute-start | bytes 5505032 | tf_op jit(solution)/shard_map/ppermute | solution.py:23
  12.8 15.4 %collective-permute-start.1 = (bf16[32,3584]{1,0:T(8,128)(2,1)}, bf16[32,3584]{1,0:T(8,128)(2,1)}, u32[]{:S(2)}, u32[]{:S(2)}) collective-permute-start(bf16[32,3584]{1,0:T(8,128)(2,1)} %get-tuple-element.52), channel_id=1, source_target_pairs={{0,0},{1,1},{2,2},{3,3},{4,4},{5,5},{6,6},{7,7},{8,8},{9,9},{10,10... | collective-permute-start | bytes 688136 | tf_op jit(solution)/shard_map/ppermute | solution.py:23
  16.1 87.1 %collective-permute-start.9 = (bf16[32,3584]{1,0:T(8,128)(2,1)S(1)}, bf16[32,3584]{1,0:T(8,128)(2,1)S(1)}, u32[]{:S(2)}, u32[]{:S(2)}) collective-permute-start(bf16[32,3584]{1,0:T(8,128)(2,1)S(1)} %get-tuple-element.45), channel_id=1, source_target_pairs={{0,28},{1,29},{2,30},{3,31},{4,0},{5,1},{6,2},{7,3},{8,4},{9,5},{1... | collective-permute-start | bytes 688136 | tf_op jit(solution)/shard_map/ppermute | solution.py:23
  22.0 80.4 %collective-permute-start.8 = (bf16[32,3584]{1,0:T(8,128)(2,1)S(1)}, bf16[32,3584]{1,0:T(8,128)(2,1)S(1)}, u32[]{:S(2)}, u32[]{:S(2)}) collective-permute-start(bf16[32,3584]{1,0:T(8,128)(2,1)S(1)} %get-tuple-element.46), channel_id=1, source_target_pairs={{0,24},{1,25},{2,26},{3,27},{4,28},{5,29},{6,30},{7,31},{8,0},{9,1... | collective-permute-start | bytes 688136 | tf_op jit(solution)/shard_map/ppermute | solution.py:23
  28.2 20.4 %collective-permute-start.2 = (bf16[32,3584]{1,0:T(8,128)(2,1)}, bf16[32,3584]{1,0:T(8,128)(2,1)S(1)}, u32[]{:S(2)}, u32[]{:S(2)}) collective-permute-start(bf16[32,3584]{1,0:T(8,128)(2,1)} %get-tuple-element.51), channel_id=1, source_target_pairs={{0,4},{1,5},{2,6},{3,7},{4,8},{5,9},{6,10},{7,11},{8,12},{9,13},{1... | collective-permute-start | bytes 688136 | tf_op jit(solution)/shard_map/ppermute | solution.py:23
  48.7 40.2 %copy-start.3 = (bf16[32,3584]{1,0:T(8,128)(2,1)S(1)}, bf16[32,3584]{1,0:T(8,128)(2,1)}, u32[]{:S(2)}) copy-start(bf16[32,3584]{1,0:T(8,128)(2,1)} %get-tuple-element.48) | copy-start | bytes 688132
  48.7 10.8 %collective-permute-start.3 = (bf16[32,3584]{1,0:T(8,128)(2,1)}, bf16[32,3584]{1,0:T(8,128)(2,1)S(1)}, u32[]{:S(2)}, u32[]{:S(2)}) collective-permute-start(bf16[32,3584]{1,0:T(8,128)(2,1)} %get-tuple-element.50), channel_id=1, source_target_pairs={{0,8},{1,9},{2,10},{3,11},{4,12},{5,13},{6,14},{7,15},{8,16},{9,17... | collective-permute-start | bytes 688136 | tf_op jit(solution)/shard_map/ppermute | solution.py:23
  59.5 42.3 %collective-permute-start.7 = (bf16[32,3584]{1,0:T(8,128)(2,1)}, bf16[32,3584]{1,0:T(8,128)(2,1)S(1)}, u32[]{:S(2)}, u32[]{:S(2)}) collective-permute-start(bf16[32,3584]{1,0:T(8,128)(2,1)} %get-tuple-element.47), channel_id=1, source_target_pairs={{0,20},{1,21},{2,22},{3,23},{4,24},{5,25},{6,26},{7,27},{8,28},{9,... | collective-permute-start | bytes 688136 | tf_op jit(solution)/shard_map/ppermute | solution.py:23
  71.8 17.1 %collective-permute-start.5 = (bf16[32,3584]{1,0:T(8,128)(2,1)}, bf16[32,3584]{1,0:T(8,128)(2,1)S(1)}, u32[]{:S(2)}, u32[]{:S(2)}) collective-permute-start(bf16[32,3584]{1,0:T(8,128)(2,1)} %get-tuple-element.49), channel_id=1, source_target_pairs={{0,12},{1,13},{2,14},{3,15},{4,16},{5,17},{6,18},{7,19},{8,20},{9,... | collective-permute-start | bytes 688136 | tf_op jit(solution)/shard_map/ppermute | solution.py:23
  88.9 12.1 %collective-permute-start.6 = (bf16[32,3584]{1,0:T(8,128)(2,1)S(1)}, bf16[32,3584]{1,0:T(8,128)(2,1)S(1)}, u32[]{:S(2)}, u32[]{:S(2)}) collective-permute-start(bf16[32,3584]{1,0:T(8,128)(2,1)S(1)} %copy-done.3), channel_id=1, source_target_pairs={{0,16},{1,17},{2,18},{3,19},{4,20},{5,21},{6,22},{7,23},{8,24},{9,... | collective-permute-start | bytes 688136 | tf_op jit(solution)/shard_map/ppermute | solution.py:23
  103.8 1.9 collective-permute-start.12
  103.8 42.7 %collective-permute-start.11 = (bf16[256,3584]{1,0:T(8,128)(2,1)}, bf16[256,3584]{1,0:T(8,128)(2,1)}, u32[]{:S(2)}, u32[]{:S(2)}) collective-permute-start(bf16[256,3584]{1,0:T(8,128)(2,1)} %constant_dynamic-update-slice_fusion), channel_id=1, source_target_pairs={{0,34},{1,35},{2,32},{3,33},{4,38},{5,39},{6,36},{7,37},{8,42},{9,... | collective-permute-start | bytes 5505032 | tf_op jit(solution)/shard_map/ppermute | solution.py:23
  105.8 40.8 %collective-permute-start.13 = (bf16[3584,256]{1,0:T(8,128)(2,1)}, bf16[3584,256]{1,0:T(8,128)(2,1)}, u32[]{:S(2)}, u32[]{:S(2)}) collective-permute-start(bf16[3584,256]{1,0:T(8,128)(2,1)} %bitcast.5), channel_id=1, source_target_pairs={{0,1},{1,0},{2,3},{3,2},{4,5},{5,4},{6,7},{7,6},{8,9},{9,8},{10,11... | collective-permute-start | bytes 5505032 | tf_op jit(solution)/shard_map/ppermute | solution.py:23
  105.9 40.7 %collective-permute-start.14 = (bf16[3584,256]{1,0:T(8,128)(2,1)}, bf16[3584,256]{1,0:T(8,128)(2,1)}, u32[]{:S(2)}, u32[]{:S(2)}) collective-permute-start(bf16[3584,256]{1,0:T(8,128)(2,1)} %bitcast.6), channel_id=1, source_target_pairs={{0,1},{1,0},{2,3},{3,2},{4,5},{5,4},{6,7},{7,6},{8,9},{9,8},{10,11... | collective-permute-start | bytes 5505032 | tf_op jit(solution)/shard_map/ppermute | solution.py:23
  106.3 51.0 %collective-permute-start.16 = (bf16[256,3584]{1,0:T(8,128)(2,1)}, bf16[256,3584]{1,0:T(8,128)(2,1)}, u32[]{:S(2)}, u32[]{:S(2)}) collective-permute-start(bf16[256,3584]{1,0:T(8,128)(2,1)} %constant_dynamic-update-slice_fusion), channel_id=1, source_target_pairs={{0,32},{1,33},{2,34},{3,35},{4,36},{5,37},{6,38},{7,39},{8,40},{9,... | collective-permute-start | bytes 5505032 | tf_op jit(solution)/shard_map/ppermute | solution.py:23
  107.5 58.5 %all-to-all-start.1 = ((bf16[8,32,3584]{2,1,0:T(8,128)(2,1)}), bf16[8,32,3584]{2,1,0:T(8,128)(2,1)}, u32[]{:S(2)}, u32[]{:S(2)}) async-start(bf16[8,32,3584]{2,1,0:T(8,128)(2,1)} %bitcast.25), calls=%async_computation.1 | async-start | bytes 3670016 | tf_op jit(solution)/shard_map/all_to_all | solution.py:74
  111.9 61.0 %collective-permute-start.18 = (bf16[256,3584]{1,0:T(8,128)(2,1)}, bf16[256,3584]{1,0:T(8,128)(2,1)}, u32[]{:S(2)}, u32[]{:S(2)}) collective-permute-start(bf16[256,3584]{1,0:T(8,128)(2,1)} %bitcast.73), channel_id=1, source_target_pairs={{0,1},{1,0},{2,3},{3,2},{4,5},{5,4},{6,7},{7,6},{8,9},{9,8},{10,11... | collective-permute-start | bytes 5505032 | tf_op jit(solution)/shard_map/ppermute | solution.py:23
  146.6 19.4 %collective-permute-start.19 = (bf16[256,3584]{1,0:T(8,128)(2,1)}, bf16[256,3584]{1,0:T(8,128)(2,1)}, u32[]{:S(2)}, u32[]{:S(2)}) collective-permute-start(bf16[256,3584]{1,0:T(8,128)(2,1)} %collective-permute-done.10), channel_id=1, source_target_pairs={{0,1},{1,0},{2,3},{3,2},{4,5},{5,4},{6,7},{7,6},{8,9},{9,8},{10,11... | collective-permute-start | bytes 5505032 | tf_op jit(solution)/shard_map/ppermute | solution.py:23
  154.5 10.7 %collective-permute-start.17 = (bf16[256,512]{1,0:T(8,128)(2,1)S(1)}, bf16[256,512]{1,0:T(8,128)(2,1)S(1)}, u32[]{:S(2)}, u32[]{:S(2)}) collective-permute-start(bf16[256,512]{1,0:T(8,128)(2,1)S(1)} %fusion.68), channel_id=1, source_target_pairs={{0,2},{1,3},{2,0},{3,1},{4,6},{5,7},{6,4},{7,5},{8,10},{9,11},{10,... | collective-permute-start | bytes 786440 | tf_op jit(solution)/shard_map/ppermute | solution.py:23
  166.0 6.9 %copy-start.8 = (bf16[1,1,256,3584]{3,2,1,0:T(8,128)(2,1)S(1)}, bf16[1,1,256,3584]{3,2,1,0:T(8,128)(2,1)}, u32[]{:S(2)}) copy-start(bf16[1,1,256,3584]{3,2,1,0:T(8,128)(2,1)} %param.21) | copy-start | bytes 5505028
  170.6 10.9 %collective-permute-start.20 = (bf16[256,512]{1,0:T(8,128)(2,1)}, bf16[256,512]{1,0:T(8,128)(2,1)}, u32[]{:S(2)}, u32[]{:S(2)}) collective-permute-start(bf16[256,512]{1,0:T(8,128)(2,1)} %fusion.44), channel_id=1, source_target_pairs={{0,2},{1,3},{2,0},{3,1},{4,6},{5,7},{6,4},{7,5},{8,10},{9,11},{10,... | collective-permute-start | bytes 786440 | tf_op jit(solution)/shard_map/ppermute | solution.py:23
  177.9 57.8 %all-to-all-start = ((bf16[8,32,3584]{2,1,0:T(8,128)(2,1)}), bf16[8,32,3584]{2,1,0:T(8,128)(2,1)S(1)}, u32[]{:S(2)}, u32[]{:S(2)}) async-start(bf16[8,32,3584]{2,1,0:T(8,128)(2,1)} %bitcast.59), calls=%async_computation | async-start | bytes 3670016 | tf_op jit(solution)/shard_map/all_to_all | solution.py:74
  186.5 43.2 %collective-permute-start.22 = (bf16[256,2560]{1,0:T(8,128)(2,1)S(1)}, bf16[256,2560]{1,0:T(8,128)(2,1)S(1)}, u32[]{:S(2)}, u32[]{:S(2)}) collective-permute-start(bf16[256,2560]{1,0:T(8,128)(2,1)S(1)} %fusion.20), channel_id=1, source_target_pairs={{0,2},{1,3},{2,0},{3,1},{4,6},{5,7},{6,4},{7,5},{8,10},{9,11},{10,... | collective-permute-start | bytes 3932168 | tf_op jit(solution)/shard_map/ppermute | solution.py:23
  191.6 28.5 %collective-permute-start.23 = (f32[256]{0:T(256)S(1)}, f32[256]{0:T(256)S(1)}, u32[]{:S(2)}, u32[]{:S(2)}) collective-permute-start(f32[256]{0:T(256)S(1)} %get-tuple-element.43), channel_id=1, source_target_pairs={{0,2},{1,3},{2,0},{3,1},{4,6},{5,7},{6,4},{7,5},{8,10},{9,11},{10,... | collective-permute-start | bytes 3080 | tf_op jit(solution)/shard_map/ppermute | solution.py:23
  196.3 33.4 %collective-permute-start.21 = (bf16[256,1024]{1,0:T(8,128)(2,1)S(1)}, bf16[256,1024]{1,0:T(8,128)(2,1)S(1)}, u32[]{:S(2)}, u32[]{:S(2)}) collective-permute-start(bf16[256,1024]{1,0:T(8,128)(2,1)S(1)} %fusion.41), channel_id=1, source_target_pairs={{0,2},{1,3},{2,0},{3,1},{4,6},{5,7},{6,4},{7,5},{8,10},{9,11},{10,... | collective-permute-start | bytes 1572872 | tf_op jit(solution)/shard_map/ppermute | solution.py:23
  235.6 8.1 %copy-start.5 = (s32[1,128,1]{1,2,0:T(1,128)S(1)}, s32[1,128,1]{1,2,0:T(1,128)}, u32[]{:S(2)}) copy-start(s32[1,128,1]{1,2,0:T(1,128)} %param.12) | copy-start | bytes 1540
  235.6 28.6 %copy-start.6 = (f32[1,128]{1,0:T(1,128)S(1)}, f32[1,128]{1,0:T(1,128)}, u32[]{:S(2)}) copy-start(f32[1,128]{1,0:T(1,128)} %param.13) | copy-start | bytes 1540
  236.8 52.2 %all-to-all-start.2 = ((bf16[8,32,3712]{2,1,0:T(8,128)(2,1)}), bf16[8,32,3712]{2,1,0:T(8,128)(2,1)S(1)}, u32[]{:S(2)}, u32[]{:S(2)}) async-start(bf16[8,32,3712]{2,1,0:T(8,128)(2,1)} %bitcast.27), calls=%async_computation.2 | async-start | bytes 3801088 | tf_op jit(solution)/shard_map/all_to_all | solution.py:74
  243.7 20.5 %collective-permute-start.15 = (bf16[128,3584]{1,0:T(8,128)(2,1)}, bf16[128,3584]{1,0:T(8,128)(2,1)}, u32[]{:S(2)}, u32[]{:S(2)}) collective-permute-start(bf16[128,3584]{1,0:T(8,128)(2,1)} %bitcast.60), channel_id=1, source_target_pairs={{0,32},{1,33},{2,34},{3,35},{4,36},{5,37},{6,38},{7,39},{8,40},{9,... | collective-permute-start | bytes 2752520 | tf_op jit(solution)/shard_map/ppermute | solution.py:23
  (5 other events, 15.9 us)
